TPU v7x, 32 devices: a whole 2x2x4 slice. The times are simulated.
32 devices in a mesh: cuts: 2 (over y), mode: 4 (over z), group: 2 (over x), batch: 2 (over core).
Axes of the slice: x: 2, y: 2, z: 4, core: 2. Of those that a mesh axis runs over, the one named last changes fastest.
Arguments:
- stem_slice: bfloat16 [2, 4, 16384, 128], P(None, ('cuts', 'batch'), ('mode', 'group')), parts along dimension 1, may hold values from -6 to 6
- column_branch: bfloat16 [2, 128, 128], replicated, may hold values from -0.375 to 0.375
- row_branch: bfloat16 [2, 128, 128], replicated, may hold values from -0.375 to 0.375
- mode_branch: bfloat16 [2, 128, 128], replicated, may hold values from -0.375 to 0.375
- final_branch: bfloat16 [2, 1024, 128], replicated, may hold values from -0.125 to 0.125
- row_labels: int32 [128], replicated, may hold values from 0 to 127, each once
- mode_labels: int32 [128], replicated, may hold values from 0 to 127, each once
- requests: int32 [2, 232], P('batch', ('mode', 'group')), may hold values from 0 to 2047, as said below
Outputs:
- amplitudes: bfloat16 [2, 4, 232, 128], P(None, ('cuts', 'batch'), ('mode', 'group')), parts along dimension 1
There are 2 independent parts, one for each index of `cuts`. A program takes and returns all parts, laid end to end along the dimension named above; an argument that names none is the same for every part. Nothing has to cross between parts.
Inputs may be any that keep to these rules, and one draw needn't show every extreme that they name: `requests`: within each set, each device's 29 entries name rows of its own batch slice; at most 8 of one device's entries name rows held by one device (index divided by 256), and some device of each set is named exactly 8 times by every device of the set. `row_labels`: a permutation. `mode_labels`: a permutation.
All inputs are finite; a program needn't handle non-finite values.
Results may differ from a plain program's by a relative error of at most 0.0064.
Values may be sent and summed in bfloat16 or wider, within the bound.
A program may use at most 64 MiB of HBM per device.

v0:
```python
import jax
import jax.numpy as jnp
from jax import lax
from jax.sharding import PartitionSpec as P

CAPACITY = 8


def complex_table(weight):
    real_part = weight[0]
    imag_part = weight[1]
    return jnp.stack([jnp.stack([real_part, imag_part], 1), jnp.stack([-imag_part, real_part], 1)])


def relabel(weight, labels):
    label_count = labels.shape[0]
    onehot = (labels[:, None] == jnp.arange(label_count, dtype=jnp.int32)[None, :]).astype(
        jnp.float32
    )
    relabelled = jnp.einsum(
        "ji,zjn->zin", onehot, weight.astype(jnp.float32), precision=lax.Precision.HIGHEST
    )
    return complex_table(relabelled.astype(jnp.bfloat16))


def per_device(
    stem_slice,
    column_branch,
    row_branch,
    mode_branch,
    final_branch,
    row_labels,
    mode_labels,
    requests,
):
    local_block = stem_slice[:, 0]
    row_count = local_block.shape[1]
    col_width = local_block.shape[2]
    first_mixed = jnp.einsum(
        "zlc,zcwk->wlk",
        local_block,
        complex_table(column_branch),
        preferred_element_type=jnp.float32,
    ).astype(jnp.bfloat16)
    grouped = first_mixed.reshape(2, row_count // col_width, col_width, col_width)
    second = jnp.einsum(
        "zgjc,zjwk->wgkc",
        grouped,
        relabel(row_branch, row_labels),
        preferred_element_type=jnp.float32,
    ).astype(jnp.bfloat16)
    peer_count = lax.axis_size(("mode", "group"))
    order_size = mode_branch.shape[1]
    sub_rows = order_size // peer_count
    blocks = row_count // order_size
    mode_table = relabel(mode_branch, mode_labels).reshape(2, peer_count, sub_rows, 2, order_size)
    shaped = second.reshape(2, peer_count, blocks, sub_rows, col_width)
    mode_mixed = jnp.einsum(
        "zqhsc,zqswk->whkc",
        lax.all_to_all(shaped, ("mode", "group"), split_axis=1, concat_axis=1, tiled=True),
        mode_table,
        preferred_element_type=jnp.float32,
    ).astype(jnp.bfloat16)
    stem_rows = mode_mixed.reshape(2, row_count // 8, 8 * col_width)
    row_total = stem_rows.shape[1]
    wanted = requests[0]
    owner_index = wanted // row_total
    row_index = wanted - owner_index * row_total
    peer_ids = jnp.arange(peer_count, dtype=jnp.int32)
    onehot = (owner_index[:, None] == peer_ids[None, :]).astype(jnp.int32)
    slot_rank = jnp.sum((jnp.cumsum(onehot, axis=0) - onehot) * onehot, axis=1)
    flat_slot = owner_index * CAPACITY + slot_rank
    send_rows = (
        jnp.full((peer_count * CAPACITY,), -1, jnp.int32)
        .at[flat_slot]
        .set(row_index)
        .reshape(peer_count, CAPACITY)
    )
    asked_rows = lax.all_to_all(
        send_rows, ("mode", "group"), split_axis=0, concat_axis=0, tiled=True
    )
    safe_rows = jnp.maximum(asked_rows, 0).reshape(-1)
    final_table = complex_table(final_branch)
    results = jnp.einsum(
        "zlr,zrwk->wlk", stem_rows, final_table, preferred_element_type=jnp.float32
    ).astype(jnp.bfloat16)
    picked = jnp.take(results, safe_rows, axis=1).reshape(2, peer_count, CAPACITY, results.shape[2])
    returned = lax.all_to_all(picked, ("mode", "group"), split_axis=1, concat_axis=1, tiled=True)
    amplitudes = jnp.take(
        returned.reshape(2, peer_count * CAPACITY, results.shape[2]), flat_slot, axis=1
    )
    return amplitudes[:, None]


def solution(mesh):
    return jax.shard_map(
        per_device,
        mesh=mesh,
        in_specs=(
            P(None, ("cuts", "batch"), ("mode", "group"), None),
            P(),
            P(),
            P(),
            P(),
            P(),
            P(),
            P("batch", ("mode", "group")),
        ),
        out_specs=P(None, ("cuts", "batch"), ("mode", "group"), None),
        check_vma=False,
    )
```

profile of v0, /device:TPU:0, one launch (start us, length us, event | category | flops | bytes accessed | tf_op | source)
XLA Modules:
  0.0 62.8 jit_solution(9416212213114320281)
XLA Ops:
  0.0 0.8 %bitcast_subtract_fusion = (s32[29]{0:T(128)S(1)}, s32[29]{0:T(128)S(1)}) fusion(s32[1,29]{1,0:T(1,128)} %param.15), kind=kLoop, calls=%fused_computation.72 | loop fusion | flops 493 | bytes 348 | tf_op jit(solution)/shard_map/sub | solution.py:68
  0.9 0.2 select_reduce_fusion
  1.1 0.7 %fusion.30 = s32[29]{0:T(128)S(1)} fusion(s32[29]{0:T(128)S(1)} %select_reduce_fusion, s32[1,29]{1,0:T(1,128)} %param.15), kind=kLoop, calls=%fused_computation.69 | loop fusion | flops 580 | bytes 348 | tf_op jit(solution)/shard_map/jit(_take)/jit(_where)/select_n | solution.py:89
  1.7 0.7 %scatter_custom_fusion = s32[64]{0:T(128)S(1)} fusion(s32[29]{0:T(128)S(1)} %fusion.30, s32[29]{0:T(128)S(1)} %get-tuple-element.5, s32[]{:T(128)} %constant.53.clone.1), kind=kCustom, calls=%fused_computation.74 | custom fusion | bytes 260 | tf_op jit(solution)/shard_map/scatter | solution.py:76
  2.4 0.7 %all_to_all.12 = s32[8,1,8]{2,0,1:T(8,128)} reshape(s32[64]{0:T(128)S(1)} %scatter_custom_fusion) | data formatting | bytes 512 | tf_op jit(solution)/shard_map/all_to_all | solution.py:79
  3.1 7.3 %all-to-all-start = ((s32[8,1,8]{2,1,0:T(1,128)}), s32[8,1,8]{2,1,0:T(1,128)S(1)}, u32[]{:S(2)}, u32[]{:S(2)}) async-start(s32[8,1,8]{2,1,0:T(1,128)} %bitcast.4), calls=%async_computation | async-start | bytes 8192 | tf_op jit(solution)/shard_map/all_to_all | solution.py:79
  10.3 1.0 %fusion.5 = bf16[2,128,128]{2,1,0:T(8,128)(2,1)S(1)} fusion(bf16[2,128,128]{2,1,0:T(8,128)(2,1)} %param.10, s32[128]{0:T(128)} %param.13), kind=kOutput, calls=%fused_computation.14 | convolution fusion | flops 8437760 | bytes 131584 | tf_op jit(solution)/shard_map/ji,zjn->zin/dot_general | solution.py:20
  11.4 0.8 %fusion.39 = (bf16[1,128,128]{2,1,0:T(8,128)(2,1)S(1)}, bf16[1,128,128]{2,1,0:T(8,128)(2,1)S(1)}) fusion(bf16[2,128,128]{2,1,0:T(8,128)(2,1)} %param.9), kind=kLoop, calls=%fused_computation.84 | loop fusion | bytes 131072 | tf_op jit(solution)/shard_map/slice | solution.py:11
  12.2 0.1 copy.70
  12.3 0.1 copy.69
  12.4 0.5 fusion
  12.9 0.2 copy.71
  13.2 0.9 %copy.51 = bf16[2,16,128,128]{3,2,0,1:T(8,128)(2,1)S(1)} copy(bf16[2,16,128,128]{2,1,3,0:T(8,128)(2,1)S(1)} %bitcast.149) | data formatting | bytes 2097152 | tf_op jit(solution)/shard_map/reshape | solution.py:45
  14.1 0.5 bitcast_convert_fusion.1
  14.6 1.2 %copy.52 = bf16[2,8,16,16,128]{4,3,0,2,1:T(8,128)(2,1)} copy(bf16[2,8,16,16,128]{4,3,2,1,0:T(8,128)(2,1)S(1)} %bitcast.147) | data formatting | bytes 2097152 | tf_op jit(solution)/shard_map/reshape | solution.py:57
  15.7 1.0 %all-to-all-done = s32[8,1,8]{2,1,0:T(1,128)S(1)} async-done(((s32[8,1,8]{2,1,0:T(1,128)}), s32[8,1,8]{2,1,0:T(1,128)S(1)}, u32[]{:S(2)}, u32[]{:S(2)}) %all-to-all-start) | async-done | bytes 288 | tf_op jit(solution)/shard_map/all_to_all | solution.py:79
  16.7 5.2 %all-to-all-start.1 = ((bf16[2,8,16,16,128]{4,3,0,2,1:T(8,128)(2,1)}), bf16[2,8,16,16,128]{4,3,0,2,1:T(8,128)(2,1)S(1)}, u32[]{:S(2)}, u32[]{:S(2)}) async-start(bf16[2,8,16,16,128]{4,3,0,2,1:T(8,128)(2,1)} %copy.52), calls=%async_computation.1 | async-start | bytes 2097152 | tf_op jit(solution)/shard_map/all_to_all | solution.py:60
  21.9 0.2 fusion.4
  22.1 0.1 copy.68
  22.3 0.1 copy.67
  22.5 1.1 %maximum_bitcast_fusion = (bf16[1,1024,2,128]{1,3,0,2:T(8,128)(2,1)}, bf16[1,1024,2,128]{1,3,0,2:T(8,128)(2,1)}) fusion(bf16[1024,1,128]{0,2,1:T(8,128)(2,1)S(1)} %bitcast.150, bf16[1024,1,128]{0,2,1:T(8,128)(2,1)S(1)} %bitcast.151, bf16[1024,1,128]{0,2,1:T(8,128)(2,1)S(1)} %bitcast_negate_fusion.1), kind=kLoop, calls=%fused_computation.22 | loop fusion | flops 524288 | bytes 1835008 | tf_op jit(solution)/shard_map/stack | solution.py:12
  23.7 23.6 %all-to-all-done.1 = bf16[2,8,16,16,128]{4,3,0,2,1:T(8,128)(2,1)S(1)} async-done(((bf16[2,8,16,16,128]{4,3,0,2,1:T(8,128)(2,1)}), bf16[2,8,16,16,128]{4,3,0,2,1:T(8,128)(2,1)S(1)}, u32[]{:S(2)}, u32[]{:S(2)}) %all-to-all-start.1) | async-done | bytes 1048608 | tf_op jit(solution)/shard_map/all_to_all | solution.py:60
  47.3 0.5 fusion.1
  47.8 0.5 reshape.250
  48.3 1.7 %fusion.3 = bf16[2,256,128]{1,2,0:T(8,128)(2,1)S(1)} fusion(bf16[2,256,1024,1]{2,1,0,3:T(8,128)(2,1)S(1)} %reshape.250, bf16[1,1024,2,128]{1,3,0,2:T(8,128)(2,1)} %get-tuple-element.10, bf16[1,1024,2,128]{1,3,0,2:T(8,128)(2,1)} %get-tuple-element.9), kind=kOutput, calls=%fused_computation.10 | convolution fusion | flops 269025280 | bytes 2228224 | tf_op jit(solution)/shard_map/zlr,zrwk->wlk/dot_general | solution.py:84
  50.0 0.1 copy.54
  50.1 0.6 %gather_fusion = bf16[64,2,128]{2,1,0:T(2,128)(2,1)S(1)} fusion(bf16[2,256,128]{2,0,1:T(2,128)(2,1)S(1)} %copy.54, s32[1024]{0:T(1024)S(1)} %pad_clamp_fusion.1), kind=kCustom, calls=%fused_computation | custom fusion | bytes 65792 | tf_op jit(solution)/shard_map/jit(_take)/gather | solution.py:87
  50.8 0.6 copy.56
  51.4 3.4 %all-to-all-start.2 = ((bf16[2,8,8,128]{3,2,0,1:T(8,128)(2,1)}), bf16[2,8,8,128]{3,2,0,1:T(8,128)(2,1)S(1)}, u32[]{:S(2)}, u32[]{:S(2)}) async-start(bf16[2,8,8,128]{3,2,0,1:T(8,128)(2,1)} %copy.56), calls=%async_computation.2 | async-start | bytes 65536 | tf_op jit(solution)/shard_map/all_to_all | solution.py:88
  54.8 6.7 %all-to-all-done.2 = bf16[2,8,8,128]{3,2,0,1:T(8,128)(2,1)S(1)} async-done(((bf16[2,8,8,128]{3,2,0,1:T(8,128)(2,1)}), bf16[2,8,8,128]{3,2,0,1:T(8,128)(2,1)S(1)}, u32[]{:S(2)}, u32[]{:S(2)}) %all-to-all-start.2) | async-done | bytes 32800 | tf_op jit(solution)/shard_map/all_to_all | solution.py:88
  61.5 0.6 gather_fusion.1
  62.1 0.7 %broadcast_select_fusion = bf16[2,1,29,128]{3,0,2,1:T(2,128)(2,1)} fusion(pred[29]{0:T(512)(128)(4,1)S(1)} %compare_and_fusion, bf16[29,2,128]{2,1,0:T(2,128)(2,1)S(1)} %gather_fusion.1), kind=kLoop, calls=%fused_computation.50 | loop fusion | flops 7424 | bytes 29725 | tf_op jit(solution)/shard_map/jit(_take)/select_n | solution.py:89
  (28 shorter events, 0.5 us)
Async XLA Ops:
  0.0 12.4 %copy-start = (bf16[2,1,2048,128]{3,2,1,0:T(8,128)(2,1)S(1)}, bf16[2,1,2048,128]{3,2,1,0:T(8,128)(2,1)}, u32[]{:S(2)}) copy-start(bf16[2,1,2048,128]{3,2,1,0:T(8,128)(2,1)} %param.8) | copy-start | bytes 3145732
  3.1 13.6 %all-to-all-start = ((s32[8,1,8]{2,1,0:T(1,128)}), s32[8,1,8]{2,1,0:T(1,128)S(1)}, u32[]{:S(2)}, u32[]{:S(2)}) async-start(s32[8,1,8]{2,1,0:T(1,128)} %bitcast.4), calls=%async_computation | async-start | bytes 8192 | tf_op jit(solution)/shard_map/all_to_all | solution.py:79
  15.7 6.2 %copy-start.2 = (bf16[2,128,128]{2,1,0:T(8,128)(2,1)S(1)}, bf16[2,128,128]{2,1,0:T(8,128)(2,1)}, u32[]{:S(2)}) copy-start(bf16[2,128,128]{2,1,0:T(8,128)(2,1)} %param.11) | copy-start | bytes 196612
  15.7 6.2 %copy-start.3 = (s32[128]{0:T(128)S(1)}, s32[128]{0:T(128)}, u32[]{:S(2)}) copy-start(s32[128]{0:T(128)} %param.14) | copy-start | bytes 1540
  15.7 6.4 %copy-start.1 = (bf16[2,1024,128]{2,1,0:T(8,128)(2,1)S(1)}, bf16[2,1024,128]{2,1,0:T(8,128)(2,1)}, u32[]{:S(2)}) copy-start(bf16[2,1024,128]{2,1,0:T(8,128)(2,1)} %param.12) | copy-start | bytes 1572868
  16.7 30.6 %all-to-all-start.1 = ((bf16[2,8,16,16,128]{4,3,0,2,1:T(8,128)(2,1)}), bf16[2,8,16,16,128]{4,3,0,2,1:T(8,128)(2,1)S(1)}, u32[]{:S(2)}, u32[]{:S(2)}) async-start(bf16[2,8,16,16,128]{4,3,0,2,1:T(8,128)(2,1)} %copy.52), calls=%async_computation.1 | async-start | bytes 2097152 | tf_op jit(solution)/shard_map/all_to_all | solution.py:60
  51.4 10.1 %all-to-all-start.2 = ((bf16[2,8,8,128]{3,2,0,1:T(8,128)(2,1)}), bf16[2,8,8,128]{3,2,0,1:T(8,128)(2,1)S(1)}, u32[]{:S(2)}, u32[]{:S(2)}) async-start(bf16[2,8,8,128]{3,2,0,1:T(8,128)(2,1)} %copy.56), calls=%async_computation.2 | async-start | bytes 65536 | tf_op jit(solution)/shard_map/all_to_all | solution.py:88
where the time goes:
time: 63.3 us; the launch traced here: 62.8 us
  waiting for transfers between devices  31.3 us (49%)
  starting transfers between devices  15.8 us (25%)
  local copies, waits for them, and re-layouts  7.6 us (12%)
  matrix products  4.23 us (7%)
  other arithmetic  3.73 us (6%)
    all_to_all x1, waiting for transfers between devices, per_device(): lax.all_to_all(shaped, ('mode', 'group'), split_axis=1, concat_axis=1, ti...  23.6 us
    all_to_all x1, starting transfers between devices, per_device(): lax.all_to_all(send_rows, ('mode', 'group'), split_axis=0, concat_axis=0,...  7.25 us
    all_to_all x1, waiting for transfers between devices, per_device(): lax.all_to_all(picked, ('mode', 'group'), split_axis=1, concat_axis=1, ti...  6.68 us
    all_to_all x1, starting transfers between devices, per_device(): lax.all_to_all(shaped, ('mode', 'group'), split_axis=1, concat_axis=1, ti...  5.15 us
    all_to_all x1, starting transfers between devices, per_device(): lax.all_to_all(picked, ('mode', 'group'), split_axis=1, concat_axis=1, ti...  3.37 us
    dot_general x1, matrix products, per_device(): jnp.einsum('zlr,zrwk->wlk', stem_rows, final_table, preferred_element_typ...  1.68 us
    select_n x2, other arithmetic, per_device(): jnp.take(returned.reshape(2, peer_count * CAPACITY, results.shape[2]), fl...  1.38 us
  transfers between devices with their start and end apart: 3, of which 3 were waited for; matrix products, arithmetic and copies ran while one was open for 11% of the time, Pallas kernels for 0%

commit v1 on v0

--- a/solution.py
+++ b/solution.py
@@ -1,9 +1,311 @@
+import functools
+
 import jax
 import jax.numpy as jnp
 from jax import lax
+from jax.experimental import pallas as pl
+from jax.experimental.pallas import tpu as pltpu
 from jax.sharding import PartitionSpec as P
 
 CAPACITY = 8
+TILE = 8
+ROWS_STEP = 2
+
+F32 = jnp.float32
+BF16 = jnp.bfloat16
+
+
+def dot(left, right):
+    return jnp.dot(left, right, preferred_element_type=F32)
+
+
+def dot_t(left, right):
+    return lax.dot_general(left, right, (((1,), (1,)), ((), ())), preferred_element_type=F32)
+
+
+def iota(shape, dim):
+    return lax.broadcasted_iota(jnp.int32, shape, dim)
+
+
+def complex_rows(real, imag, axis):
+    return jnp.concatenate([real, -imag], axis), jnp.concatenate([imag, real], axis)
+
+
+def fused_kernel(
+    mode_size,
+    group_size,
+    stem_hbm,
+    column_hbm,
+    row_hbm,
+    mode_hbm,
+    final_hbm,
+    row_labels_hbm,
+    mode_labels_hbm,
+    requests_hbm,
+    out_ref,
+    stem,
+    column,
+    row,
+    mode,
+    final,
+    row_labels,
+    mode_labels,
+    wanted,
+    asked,
+    spread,
+    picked,
+    coeffs,
+    partial,
+    outgoing,
+    incoming,
+    load_sem,
+    stem_sem,
+    ask_send,
+    ask_recv,
+    give_send,
+    give_recv,
+):
+    peers = mode_size * group_size
+    row_count, width = stem.shape[1], stem.shape[2]
+    row_order = row.shape[1]
+    order = mode.shape[1]
+    sub = order // peers
+    heads = row_order // sub
+    groups = row_count // row_order
+    length = final.shape[1]
+    fold = length // width
+    out_width = final.shape[2]
+    count = wanted.shape[1]
+    padded = outgoing.shape[1]
+    total = peers * padded
+    blocks = row_count // sub
+    row_blocks = order // fold
+    terms = 2 * sub
+    span = terms * TILE
+
+    mode_index = lax.axis_index("mode")
+    group_index = lax.axis_index("group")
+    me = mode_index * group_size + group_index
+
+    def device(offset):
+        peer = lax.rem(me + offset, peers)
+        return {"mode": peer // group_size, "group": lax.rem(peer, group_size)}
+
+    barrier = pltpu.get_barrier_semaphore()
+    for offset in range(1, peers):
+        pl.semaphore_signal(
+            barrier, inc=1, device_id=device(offset), device_id_type=pl.DeviceIdType.MESH
+        )
+
+    small = [
+        pltpu.make_async_copy(source, target, load_sem.at[index])
+        for index, (source, target) in enumerate(
+            (
+                (requests_hbm, wanted),
+                (column_hbm, column),
+                (row_hbm, row),
+                (row_labels_hbm, row_labels),
+                (mode_hbm, mode),
+                (mode_labels_hbm, mode_labels),
+                (final_hbm, final),
+            )
+        )
+    ]
+    step_rows = ROWS_STEP * row_order
+    stem_loads = [
+        pltpu.make_async_copy(
+            stem_hbm.at[:, 0, pl.ds(step * step_rows, step_rows), :],
+            stem.at[:, pl.ds(step * step_rows, step_rows), :],
+            stem_sem.at[step],
+        )
+        for step in range(groups // ROWS_STEP)
+    ]
+    for load in small[:-1]:
+        load.start()
+    for load in stem_loads:
+        load.start()
+    small[-1].start()
+
+    small[0].wait()
+    asked[0:1, :] = jnp.zeros((1, width), jnp.int32)
+    asked[0:1, 0:count] = wanted[...]
+    pl.semaphore_wait(barrier, peers - 1)
+    asks = [
+        pltpu.make_async_remote_copy(
+            src_ref=asked.at[pl.ds(0, 1), :],
+            dst_ref=asked.at[pl.ds(offset, 1), :],
+            send_sem=ask_send.at[offset],
+            recv_sem=ask_recv.at[offset],
+            device_id=device(offset),
+            device_id_type=pl.DeviceIdType.MESH,
+        )
+        for offset in range(1, peers)
+    ]
+    for ask in asks:
+        ask.start()
+
+    for load in small[1:4]:
+        load.wait()
+    column_real, column_imag = complex_rows(column[0], column[1], 0)
+    column_table = jnp.concatenate([column_real, column_imag], 1)
+    chosen = (iota((row_order, row_order), 0) == row_labels[...]).astype(BF16)
+    order_out = iota((row_order, row_order), 0)
+    order_in = iota((row_order, row_order), 1)
+    swap_rows = (
+        order_in == lax.rem(order_out, heads) * sub + lax.div(order_out, heads)
+    ).astype(BF16)
+    row_real = dot_t(swap_rows, dot(chosen, row[0]).astype(BF16)).astype(BF16)
+    row_imag = dot_t(swap_rows, dot(chosen, row[1]).astype(BF16)).astype(BF16)
+    row_table = jnp.concatenate(complex_rows(row_real, row_imag, 1), 0)
+
+    for step in range(groups // ROWS_STEP):
+        stem_loads[step].wait()
+        rows = pl.ds(step * step_rows, step_rows)
+        operand = jnp.concatenate([stem[0, rows, :], stem[1, rows, :]], 1)
+        mixed = dot(operand, column_table).astype(BF16)
+        pieces = []
+        for index in range(ROWS_STEP):
+            piece = mixed[index * row_order : (index + 1) * row_order]
+            pieces.append(jnp.concatenate([piece[:, :width], piece[:, width:]], 0))
+        result = dot(row_table, jnp.concatenate(pieces, 1))
+        for index in range(ROWS_STEP):
+            first = (step * ROWS_STEP + index) * heads
+            spread[:, first : first + heads, :] = result[
+                :, index * width : (index + 1) * width
+            ].reshape(terms, heads, width)
+
+    for load in small[4:6]:
+        load.wait()
+    own = (iota((sub, order), 0) + me * sub == mode_labels[...]).astype(BF16)
+    mode_real, mode_imag = dot(own, mode[0]), dot(own, mode[1])
+    repeat = (lax.div(iota((span, terms), 0), TILE) == iota((span, terms), 1)).astype(BF16)
+    mode_table = jnp.concatenate(
+        [dot(repeat, half.astype(BF16)) for half in complex_rows(mode_real, mode_imag, 0)], 0
+    ).astype(BF16)
+
+    for ask in asks:
+        ask.wait()
+    ids = asked[...]
+    block_ids = jnp.transpose(lax.div(ids, row_blocks).astype(F32))
+    order_ids = jnp.transpose((lax.rem(ids, row_blocks) * fold).astype(F32))
+
+    def column_of(values, lanes):
+        return jnp.concatenate(
+            [
+                jnp.broadcast_to(values[:padded, slot : slot + 1], (padded, lanes))
+                for slot in range(peers)
+            ],
+            0,
+        )
+
+    lane = iota((total, blocks), 1).astype(F32)
+    pick = (column_of(block_ids, blocks) == lane).astype(BF16)
+    for term in range(0, terms, 2):
+        pair = jnp.concatenate([spread[term], spread[term + 1]], 1).astype(BF16)
+        found = dot(pick, pair)
+        picked[term] = found[:, :width]
+        picked[term + 1] = found[:, width:]
+
+    order_column = column_of(order_ids, order)
+    lane = iota((total, order), 1).astype(F32)
+    same = lax.rem(iota((total, 2 * span), 0), TILE) == lax.rem(iota((total, 2 * span), 1), TILE)
+    for index in range(fold):
+        at = (order_column + float(index) == lane).astype(BF16)
+        values = jnp.where(same, dot_t(at, mode_table), 0.0)
+        coeffs[index] = values[:, :span]
+        coeffs[fold + index] = values[:, span:]
+
+    for tile in range(total // TILE):
+        rows = pl.ds(tile * TILE, TILE)
+        left = coeffs[:, rows, :].reshape(2 * fold * TILE, span).astype(BF16)
+        right = picked[:, rows, :].reshape(span, width).astype(BF16)
+        partial[:, rows, :] = dot(left, right).reshape(2 * fold, TILE, width)
+
+    small[6].wait()
+    halves = []
+    for half in range(2):
+        halves.append(
+            jnp.concatenate(
+                [partial[half * fold + index].astype(BF16) for index in range(fold)], 1
+            )
+        )
+    products = dot(halves[0], jnp.concatenate([final[0], final[1]], 1)) + dot(
+        halves[1], jnp.concatenate([-final[1], final[0]], 1)
+    )
+    outgoing[...] = products.reshape(peers, padded, 2 * out_width).astype(BF16)
+
+    gives = [
+        pltpu.make_async_remote_copy(
+            src_ref=outgoing.at[offset],
+            dst_ref=incoming.at[offset],
+            send_sem=give_send.at[offset],
+            recv_sem=give_recv.at[offset],
+            device_id=device(peers - offset),
+            device_id_type=pl.DeviceIdType.MESH,
+        )
+        for offset in range(1, peers)
+    ]
+    for give in gives:
+        give.start()
+    answer = products[:padded]
+    for offset, give in enumerate(gives, 1):
+        give.wait_recv()
+        answer = answer + incoming[offset].astype(F32)
+    answer = answer.astype(out_ref.dtype)
+    out_ref[0, 0] = answer[:count, :out_width]
+    out_ref[1, 0] = answer[:count, out_width:]
+    for give in gives:
+        give.wait_send()
+
+
+def fused(mode_size, group_size, padded, arguments):
+    stem_slice, column, row, mode, final, row_labels, mode_labels, requests = arguments
+    peers = mode_size * group_size
+    row_count, width = stem_slice.shape[2:]
+    order = mode.shape[1]
+    sub = order // peers
+    fold = final.shape[1] // width
+    out_width = final.shape[2]
+    count = requests.shape[1]
+    total = peers * padded
+    terms = 2 * sub
+    span = terms * TILE
+    steps = row_count // row.shape[1] // ROWS_STEP
+    row_labels = row_labels.reshape(1, -1)
+    mode_labels = mode_labels.reshape(1, -1)
+    dma = pltpu.SemaphoreType.DMA
+    return pl.pallas_call(
+        functools.partial(fused_kernel, mode_size, group_size),
+        out_shape=jax.ShapeDtypeStruct((2, 1, count, out_width), BF16),
+        in_specs=[pl.BlockSpec(memory_space=pltpu.HBM)] * 8,
+        out_specs=pl.BlockSpec(memory_space=pltpu.VMEM),
+        scratch_shapes=[
+            pltpu.VMEM((2, row_count, width), BF16),
+            pltpu.VMEM(column.shape, BF16),
+            pltpu.VMEM(row.shape, BF16),
+            pltpu.VMEM(mode.shape, BF16),
+            pltpu.VMEM(final.shape, BF16),
+            pltpu.VMEM(row_labels.shape, jnp.int32),
+            pltpu.VMEM(mode_labels.shape, jnp.int32),
+            pltpu.VMEM(requests.shape, jnp.int32),
+            pltpu.VMEM((peers, width), jnp.int32),
+            pltpu.VMEM((terms, row_count // sub, width), F32),
+            pltpu.VMEM((terms, total, width), F32),
+            pltpu.VMEM((2 * fold, total, span), F32),
+            pltpu.VMEM((2 * fold, total, width), F32),
+            pltpu.VMEM((peers, padded, 2 * out_width), BF16),
+            pltpu.VMEM((peers, padded, 2 * out_width), BF16),
+            dma((7,)),
+            dma((steps,)),
+            dma((peers,)),
+            dma((peers,)),
+            dma((peers,)),
+            dma((peers,)),
+        ],
+        compiler_params=pltpu.CompilerParams(
+            collective_id=0, has_side_effects=True, vmem_limit_bytes=48 * 1024 * 1024
+        ),
+    )(stem_slice, column, row, mode, final, row_labels, mode_labels, requests)
 
 
 def complex_table(weight):
@@ -23,7 +325,7 @@
     return complex_table(relabelled.astype(jnp.bfloat16))
 
 
-def per_device(
+def swapped(
     stem_slice,
     column_branch,
     row_branch,
@@ -92,9 +394,27 @@
     return amplitudes[:, None]
 
 
+def per_device(mode_size, group_size, *arguments):
+    stem_slice, _, row, mode, final, _, _, requests = arguments
+    peers = mode_size * group_size
+    row_count, width = stem_slice.shape[2:]
+    padded = -(-requests.shape[1] // 16) * 16
+    fits = (
+        peers == TILE
+        and padded <= width
+        and row.shape[1] == width
+        and mode.shape[1] % (16 * peers) == 0
+        and row_count % (ROWS_STEP * width) == 0
+        and 2 * peers * padded * final.shape[2] < stem_slice.size
+    )
+    if fits:
+        return fused(mode_size, group_size, padded, arguments)
+    return swapped(*arguments)
+
+
 def solution(mesh):
     return jax.shard_map(
-        per_device,
+        functools.partial(per_device, mesh.shape["mode"], mesh.shape["group"]),
         mesh=mesh,
         in_specs=(
             P(None, ("cuts", "batch"), ("mode", "group"), None),

time: 63.3 us -> 24.3 us (0.38)
  waiting for transfers between devices: 31.3 us -> 0 us
  Pallas kernels: 0 us -> 17.9 us
  starting transfers between devices: 15.8 us -> 0 us
  matrix products: 4.23 us -> 0 us
  other arithmetic: 3.73 us -> 0 us
  local copies, waits for them, and re-layouts: 7.6 us -> 6.08 us
    all_to_all x3 -> x0, waiting for transfers between devices: 31.3 us -> none  [the longest x1 23.6 us: per_device(): lax.all_to_all(shaped, ('mode', 'group'), split_axis=1, concat_axis=1, ti...]
    pallas_call x0 -> x1, Pallas kernels: none -> 17.9 us  [fused(): pl.pallas_call(functools.partial(fused_kernel, mode_size, group_size), ou...]
    all_to_all x3 -> x0, starting transfers between devices: 15.8 us -> none  [the longest x1 7.25 us: per_device(): lax.all_to_all(send_rows, ('mode', 'group'), split_axis=0, concat_axis=0,...]
    unnamed x13 -> x16, local copies, waits for them, and re-layouts: 0.76 us -> 5.47 us
    dot_general x6 -> x0, matrix products: 4.23 us -> none  [the longest x1 1.68 us: per_device(): jnp.einsum('zlr,zrwk->wlk', stem_rows, final_table, preferred_element_typ...]
    reshape x4 -> x0, local copies, waits for them, and re-layouts: 2.6 us -> none  [the longest x1 1.16 us: per_device(): shaped = second.reshape(2, peer_count, blocks, sub_rows, col_width)]
    select_n x3 -> x0, other arithmetic: 1.45 us -> none  [the longest x2 1.38 us: per_device(): jnp.take(returned.reshape(2, peer_count * CAPACITY, results.shape[2]), fl...]
    gather x2 -> x0, local copies, waits for them, and re-layouts: 1.24 us -> none  [the longest x1 0.65 us: per_device(): jnp.take(results, safe_rows, axis=1)]
  transfers between devices with their start and end apart: 3 -> 0, of which waited for: 3 -> 0; matrix products, arithmetic and copies ran while one was open for 11% -> 0% of each run, Pallas kernels for 0% -> 0%
where the time goes in v1:
time: 24.3 us; the launch traced here: 24 us
  Pallas kernels  17.9 us (74%)
  local copies, waits for them, and re-layouts  6.08 us (25%)
    pallas_call x1, Pallas kernels, fused(): pl.pallas_call(functools.partial(fused_kernel, mode_size, group_size), ou...  17.9 us
    unnamed x16, local copies, waits for them, and re-layouts  5.47 us
    pallas_call x1, local copies, waits for them, and re-layouts, fused(): pl.pallas_call(functools.partial(fused_kernel, mode_size, group_size), ou...  0.61 us

profile of v1, /device:TPU:0, one launch (start us, length us, event | category | flops | bytes accessed | tf_op | source)
XLA Modules:
  0.0 24.0 jit_solution(6938222395931898419)
XLA Ops:
  0.0 0.0 copy-start.5
  0.0 0.0 copy-start.6
  0.0 0.0 copy-start.7
  0.0 0.6 %copy-done.5 = s32[128]{0:T(128)S(1)} copy-done((s32[128]{0:T(128)S(1)}, s32[128]{0:T(128)}, u32[]{:S(2)}) %copy-start.5) | copy-done | bytes 536
  0.7 0.0 copy-done.6
  0.7 0.0 copy-done.7
  0.7 0.0 copy-start
  0.7 1.2 %copy-done = bf16[2,1,2048,128]{3,2,1,0:T(8,128)(2,1)S(1)} copy-done((bf16[2,1,2048,128]{3,2,1,0:T(8,128)(2,1)S(1)}, bf16[2,1,2048,128]{3,2,1,0:T(8,128)(2,1)}, u32[]{:S(2)}) %copy-start) | copy-done | bytes 1048600
  1.9 0.0 copy-start.1
  1.9 1.0 %copy-done.1 = bf16[2,1024,128]{2,1,0:T(8,128)(2,1)S(1)} copy-done((bf16[2,1024,128]{2,1,0:T(8,128)(2,1)S(1)}, bf16[2,1024,128]{2,1,0:T(8,128)(2,1)}, u32[]{:S(2)}) %copy-start.1) | copy-done | bytes 524312
  3.0 0.0 copy-start.2
  3.0 0.8 %copy-done.2 = bf16[2,128,128]{2,1,0:T(8,128)(2,1)S(1)} copy-done((bf16[2,128,128]{2,1,0:T(8,128)(2,1)S(1)}, bf16[2,128,128]{2,1,0:T(8,128)(2,1)}, u32[]{:S(2)}) %copy-start.2) | copy-done | bytes 65560
  3.8 0.0 copy-start.3
  3.8 0.8 %copy-done.3 = bf16[2,128,128]{2,1,0:T(8,128)(2,1)S(1)} copy-done((bf16[2,128,128]{2,1,0:T(8,128)(2,1)S(1)}, bf16[2,128,128]{2,1,0:T(8,128)(2,1)}, u32[]{:S(2)}) %copy-start.3) | copy-done | bytes 65560
  4.6 0.0 copy-start.4
  4.6 0.8 %copy-done.4 = bf16[2,128,128]{2,1,0:T(8,128)(2,1)S(1)} copy-done((bf16[2,128,128]{2,1,0:T(8,128)(2,1)S(1)}, bf16[2,128,128]{2,1,0:T(8,128)(2,1)}, u32[]{:S(2)}) %copy-start.4) | copy-done | bytes 65560
  5.5 17.9 %shard_map.82 = bf16[2,1,29,128]{3,2,1,0:T(8,128)(2,1)S(1)} custom-call(bf16[2,1,2048,128]{3,2,1,0:T(8,128)(2,1)S(1)} %copy-done, bf16[2,128,128]{2,1,0:T(8,128)(2,1)S(1)} %copy-done.2, bf16[2,128,128]{2,1,0:T(8,128)(2,1)S(1)} %copy-done.3, bf16[2,128,128]{2,1,0:T(8,128)(2,1)S(1)} %copy-done.4, bf16[2,1024,128]{2,1,0:T(8,128)(2,1)S(1)} %copy-done.1, ...), custom_call_target="tpu_custom_call" | custom-call | tf_op jit(solution)/shard_map/pallas_call | solution.py:277
  23.4 0.6 %copy.9 = bf16[2,1,29,128]{3,0,2,1:T(2,128)(2,1)} copy(bf16[2,1,29,128]{3,2,1,0:T(8,128)(2,1)S(1)} %shard_map.82) | data formatting | bytes 29696 | tf_op jit(solution)/shard_map/pallas_call | solution.py:277
Async XLA Ops:
  0.0 0.7 %copy-start.5 = (s32[128]{0:T(128)S(1)}, s32[128]{0:T(128)}, u32[]{:S(2)}) copy-start(s32[128]{0:T(128)} %param.13) | copy-start | bytes 1540
  0.0 0.7 %copy-start.6 = (s32[128]{0:T(128)S(1)}, s32[128]{0:T(128)}, u32[]{:S(2)}) copy-start(s32[128]{0:T(128)} %param.14) | copy-start | bytes 1540
  0.0 0.7 %copy-start.7 = (s32[1,29]{1,0:T(1,128)S(1)}, s32[1,29]{1,0:T(1,128)}, u32[]{:S(2)}) copy-start(s32[1,29]{1,0:T(1,128)} %requests_hbm.1) | copy-start | bytes 352
  0.7 1.2 %copy-start = (bf16[2,1,2048,128]{3,2,1,0:T(8,128)(2,1)S(1)}, bf16[2,1,2048,128]{3,2,1,0:T(8,128)(2,1)}, u32[]{:S(2)}) copy-start(bf16[2,1,2048,128]{3,2,1,0:T(8,128)(2,1)} %stem_hbm.1) | copy-start | bytes 3145732
  1.9 1.0 %copy-start.1 = (bf16[2,1024,128]{2,1,0:T(8,128)(2,1)S(1)}, bf16[2,1024,128]{2,1,0:T(8,128)(2,1)}, u32[]{:S(2)}) copy-start(bf16[2,1024,128]{2,1,0:T(8,128)(2,1)} %final_hbm.1) | copy-start | bytes 1572868
  3.0 0.8 %copy-start.2 = (bf16[2,128,128]{2,1,0:T(8,128)(2,1)S(1)}, bf16[2,128,128]{2,1,0:T(8,128)(2,1)}, u32[]{:S(2)}) copy-start(bf16[2,128,128]{2,1,0:T(8,128)(2,1)} %column_hbm.1) | copy-start | bytes 196612
  3.8 0.8 %copy-start.3 = (bf16[2,128,128]{2,1,0:T(8,128)(2,1)S(1)}, bf16[2,128,128]{2,1,0:T(8,128)(2,1)}, u32[]{:S(2)}) copy-start(bf16[2,128,128]{2,1,0:T(8,128)(2,1)} %row_hbm.1) | copy-start | bytes 196612
  4.6 0.8 %copy-start.4 = (bf16[2,128,128]{2,1,0:T(8,128)(2,1)S(1)}, bf16[2,128,128]{2,1,0:T(8,128)(2,1)}, u32[]{:S(2)}) copy-start(bf16[2,128,128]{2,1,0:T(8,128)(2,1)} %mode_hbm.1) | copy-start | bytes 196612

commit v2 on v1

--- a/solution.py
+++ b/solution.py
@@ -120,29 +120,12 @@
         )
         for step in range(groups // ROWS_STEP)
     ]
-    for load in small[:-1]:
+    for load in small[:4] + stem_loads + small[4:]:
         load.start()
-    for load in stem_loads:
-        load.start()
-    small[-1].start()
 
     small[0].wait()
     asked[0:1, :] = jnp.zeros((1, width), jnp.int32)
     asked[0:1, 0:count] = wanted[...]
-    pl.semaphore_wait(barrier, peers - 1)
-    asks = [
-        pltpu.make_async_remote_copy(
-            src_ref=asked.at[pl.ds(0, 1), :],
-            dst_ref=asked.at[pl.ds(offset, 1), :],
-            send_sem=ask_send.at[offset],
-            recv_sem=ask_recv.at[offset],
-            device_id=device(offset),
-            device_id_type=pl.DeviceIdType.MESH,
-        )
-        for offset in range(1, peers)
-    ]
-    for ask in asks:
-        ask.start()
 
     for load in small[1:4]:
         load.wait()
@@ -157,6 +140,21 @@
     row_real = dot_t(swap_rows, dot(chosen, row[0]).astype(BF16)).astype(BF16)
     row_imag = dot_t(swap_rows, dot(chosen, row[1]).astype(BF16)).astype(BF16)
     row_table = jnp.concatenate(complex_rows(row_real, row_imag, 1), 0)
+
+    pl.semaphore_wait(barrier, peers - 1)
+    asks = [
+        pltpu.make_async_remote_copy(
+            src_ref=asked.at[pl.ds(0, 1), :],
+            dst_ref=asked.at[pl.ds(offset, 1), :],
+            send_sem=ask_send.at[offset],
+            recv_sem=ask_recv.at[offset],
+            device_id=device(offset),
+            device_id_type=pl.DeviceIdType.MESH,
+        )
+        for offset in range(1, peers)
+    ]
+    for ask in asks:
+        ask.start()
 
     for step in range(groups // ROWS_STEP):
         stem_loads[step].wait()
@@ -303,7 +301,7 @@
             dma((peers,)),
         ],
         compiler_params=pltpu.CompilerParams(
-            collective_id=0, has_side_effects=True, vmem_limit_bytes=48 * 1024 * 1024
+            collective_id=0, has_side_effects=True, vmem_limit_bytes=60 * 1024 * 1024
         ),
     )(stem_slice, column, row, mode, final, row_labels, mode_labels, requests)
 

time: 24.3 us -> 20.1 us (0.83)
  local copies, waits for them, and re-layouts: 6.08 us -> 1.33 us
  Pallas kernels: 17.9 us -> 18.5 us
    unnamed x16 -> x0, local copies, waits for them, and re-layouts: 5.47 us -> none
    pallas_call x1, local copies, waits for them, and re-layouts: 0.61 us -> 1.33 us  [fused(): pl.pallas_call(functools.partial(fused_kernel, mode_size, group_size), ou...]
    pallas_call x1, Pallas kernels: 17.9 us -> 18.5 us  [fused(): pl.pallas_call(functools.partial(fused_kernel, mode_size, group_size), ou...]
where the time goes in v2:
time: 20.1 us; the launch traced here: 19.8 us
  Pallas kernels  18.5 us (92%)
  local copies, waits for them, and re-layouts  1.33 us (7%)
    pallas_call x1, Pallas kernels, fused(): pl.pallas_call(functools.partial(fused_kernel, mode_size, group_size), ou...  18.5 us
    pallas_call x1, local copies, waits for them, and re-layouts, fused(): pl.pallas_call(functools.partial(fused_kernel, mode_size, group_size), ou...  1.33 us

profile of v2, /device:TPU:0, one launch (start us, length us, event | category | flops | bytes accessed | tf_op | source)
XLA Modules:
  0.0 19.8 jit_solution(4823791105905733036)
XLA Ops:
  0.0 18.5 %shard_map.82 = bf16[2,1,29,128]{3,2,1,0:T(8,128)(2,1)} custom-call(bf16[2,1,2048,128]{3,2,1,0:T(8,128)(2,1)} %stem_hbm.1, bf16[2,128,128]{2,1,0:T(8,128)(2,1)} %column_hbm.1, bf16[2,128,128]{2,1,0:T(8,128)(2,1)} %row_hbm.1, bf16[2,128,128]{2,1,0:T(8,128)(2,1)} %mode_hbm.1, bf16[2,1024,128]{2,1,0:T(8,128)(2,1)} %final_hbm.1, s32[1,128]{1,0:T(1,128)} %bitcast.2, ...), custom_call_target="tpu_custom_call" | custom-call | tf_op jit(solution)/shard_map/pallas_call | solution.py:275
  18.5 1.3 %copy.9 = bf16[2,1,29,128]{3,0,2,1:T(2,128)(2,1)} copy(bf16[2,1,29,128]{3,2,1,0:T(8,128)(2,1)} %shard_map.82) | data formatting | bytes 29696 | tf_op jit(solution)/shard_map/pallas_call | solution.py:275

commit v3 on v2

--- a/solution.py
+++ b/solution.py
@@ -82,6 +82,7 @@
     row_blocks = order // fold
     terms = 2 * sub
     span = terms * TILE
+    tiles = total // TILE
 
     mode_index = lax.axis_index("mode")
     group_index = lax.axis_index("group")
@@ -126,20 +127,42 @@
     small[0].wait()
     asked[0:1, :] = jnp.zeros((1, width), jnp.int32)
     asked[0:1, 0:count] = wanted[...]
-
-    for load in small[1:4]:
+    for load in small[1:4] + stem_loads:
         load.wait()
+
     column_real, column_imag = complex_rows(column[0], column[1], 0)
     column_table = jnp.concatenate([column_real, column_imag], 1)
     chosen = (iota((row_order, row_order), 0) == row_labels[...]).astype(BF16)
-    order_out = iota((row_order, row_order), 0)
-    order_in = iota((row_order, row_order), 1)
+    cube = (sub, heads, row_order)
     swap_rows = (
-        order_in == lax.rem(order_out, heads) * sub + lax.div(order_out, heads)
-    ).astype(BF16)
+        (iota(cube, 1) * sub + iota(cube, 0) == iota(cube, 2))
+        .astype(F32)
+        .reshape(row_order, row_order)
+        .astype(BF16)
+    )
     row_real = dot_t(swap_rows, dot(chosen, row[0]).astype(BF16)).astype(BF16)
     row_imag = dot_t(swap_rows, dot(chosen, row[1]).astype(BF16)).astype(BF16)
     row_table = jnp.concatenate(complex_rows(row_real, row_imag, 1), 0)
+
+    def mix(step):
+        rows = pl.ds(step * step_rows, step_rows)
+        operand = jnp.concatenate([stem[0, rows, :], stem[1, rows, :]], 1)
+        mixed = dot(operand, column_table).astype(BF16)
+        pieces = []
+        for index in range(ROWS_STEP):
+            piece = mixed[index * row_order : (index + 1) * row_order]
+            pieces.append(jnp.concatenate([piece[:, :width], piece[:, width:]], 0))
+        result = dot(row_table, jnp.concatenate(pieces, 1))
+        result = [
+            result[:, index * width : (index + 1) * width].reshape(terms, heads, width)
+            for index in range(ROWS_STEP)
+        ]
+        first = step * ROWS_STEP * heads
+        spread[:, first : first + ROWS_STEP * heads, :] = jnp.concatenate(result, 1).astype(BF16)
+
+    steps = groups // ROWS_STEP
+    for step in range(steps // 2):
+        mix(step)
 
     pl.semaphore_wait(barrier, peers - 1)
     asks = [
@@ -155,34 +178,22 @@
     ]
     for ask in asks:
         ask.start()
-
-    for step in range(groups // ROWS_STEP):
-        stem_loads[step].wait()
-        rows = pl.ds(step * step_rows, step_rows)
-        operand = jnp.concatenate([stem[0, rows, :], stem[1, rows, :]], 1)
-        mixed = dot(operand, column_table).astype(BF16)
-        pieces = []
-        for index in range(ROWS_STEP):
-            piece = mixed[index * row_order : (index + 1) * row_order]
-            pieces.append(jnp.concatenate([piece[:, :width], piece[:, width:]], 0))
-        result = dot(row_table, jnp.concatenate(pieces, 1))
-        for index in range(ROWS_STEP):
-            first = (step * ROWS_STEP + index) * heads
-            spread[:, first : first + heads, :] = result[
-                :, index * width : (index + 1) * width
-            ].reshape(terms, heads, width)
-
-    for load in small[4:6]:
+    for load in small[4:]:
         load.wait()
+
+    for step in range(steps // 2, steps):
+        mix(step)
+
     own = (iota((sub, order), 0) + me * sub == mode_labels[...]).astype(BF16)
     mode_real, mode_imag = dot(own, mode[0]), dot(own, mode[1])
-    repeat = (lax.div(iota((span, terms), 0), TILE) == iota((span, terms), 1)).astype(BF16)
+    cube = (terms, TILE, terms)
+    repeat = (iota(cube, 0) == iota(cube, 2)).astype(F32).reshape(span, terms).astype(BF16)
     mode_table = jnp.concatenate(
         [dot(repeat, half.astype(BF16)) for half in complex_rows(mode_real, mode_imag, 0)], 0
     ).astype(BF16)
 
     for ask in asks:
-        ask.wait()
+        ask.wait_recv()
     ids = asked[...]
     block_ids = jnp.transpose(lax.div(ids, row_blocks).astype(F32))
     order_ids = jnp.transpose((lax.rem(ids, row_blocks) * fold).astype(F32))
@@ -196,41 +207,49 @@
             0,
         )
 
+    def paired(first, second):
+        lanes = first.shape[1]
+        both = [part.reshape(tiles, TILE, lanes) for part in (first, second)]
+        return jnp.concatenate(both, 1).astype(BF16)
+
     lane = iota((total, blocks), 1).astype(F32)
     pick = (column_of(block_ids, blocks) == lane).astype(BF16)
     for term in range(0, terms, 2):
-        pair = jnp.concatenate([spread[term], spread[term + 1]], 1).astype(BF16)
-        found = dot(pick, pair)
-        picked[term] = found[:, :width]
-        picked[term + 1] = found[:, width:]
+        found = dot(pick, jnp.concatenate([spread[term], spread[term + 1]], 1))
+        picked[:, term * TILE : (term + 2) * TILE, :] = paired(found[:, :width], found[:, width:])
 
     order_column = column_of(order_ids, order)
     lane = iota((total, order), 1).astype(F32)
-    same = lax.rem(iota((total, 2 * span), 0), TILE) == lax.rem(iota((total, 2 * span), 1), TILE)
-    for index in range(fold):
+    same = (iota((TILE, 2 * span), 1) & (TILE - 1)) == iota((TILE, 2 * span), 0)
+    same = jnp.broadcast_to(same[None], (tiles, TILE, 2 * span)).reshape(total, 2 * span)
+
+    def coefficients(index):
         at = (order_column + float(index) == lane).astype(BF16)
-        values = jnp.where(same, dot_t(at, mode_table), 0.0)
-        coeffs[index] = values[:, :span]
-        coeffs[fold + index] = values[:, span:]
-
-    for tile in range(total // TILE):
-        rows = pl.ds(tile * TILE, TILE)
-        left = coeffs[:, rows, :].reshape(2 * fold * TILE, span).astype(BF16)
-        right = picked[:, rows, :].reshape(span, width).astype(BF16)
-        partial[:, rows, :] = dot(left, right).reshape(2 * fold, TILE, width)
-
-    small[6].wait()
-    halves = []
-    for half in range(2):
-        halves.append(
-            jnp.concatenate(
-                [partial[half * fold + index].astype(BF16) for index in range(fold)], 1
-            )
-        )
-    products = dot(halves[0], jnp.concatenate([final[0], final[1]], 1)) + dot(
-        halves[1], jnp.concatenate([-final[1], final[0]], 1)
-    )
-    outgoing[...] = products.reshape(peers, padded, 2 * out_width).astype(BF16)
+        return jnp.where(same, dot_t(at, mode_table), 0.0)
+
+    for index in range(0, fold, 2):
+        first, second = coefficients(index), coefficients(index + 1)
+        for half in range(2):
+            rows = (half * fold + index) * TILE
+            lanes = slice(half * span, (half + 1) * span)
+            coeffs[:, rows : rows + 2 * TILE, :] = paired(first[:, lanes], second[:, lanes])
+
+    final_real = jnp.concatenate([final[0], final[1]], 1)
+    final_imag = jnp.concatenate([-final[1], final[0]], 1)
+
+    def products(first_slot, last_slot):
+        first, last = first_slot * padded, last_slot * padded
+        for row_start in range(first, last, 2 * TILE):
+            tile = row_start // TILE
+            both = [
+                dot(coeffs[tile + index], picked[tile + index]).reshape(2 * fold, TILE, width)
+                for index in range(2)
+            ]
+            partial[:, row_start : row_start + 2 * TILE, :] = jnp.concatenate(both, 1).astype(BF16)
+        rows = slice(first, last)
+        real = jnp.concatenate([partial[index, rows] for index in range(fold)], 1)
+        imag = jnp.concatenate([partial[fold + index, rows] for index in range(fold)], 1)
+        return dot(real, final_real) + dot(imag, final_imag)
 
     gives = [
         pltpu.make_async_remote_copy(
@@ -243,17 +262,24 @@
         )
         for offset in range(1, peers)
     ]
-    for give in gives:
+    middle = peers // 2
+    result = products(middle, peers)
+    outgoing[middle:] = result.reshape(peers - middle, padded, 2 * out_width).astype(BF16)
+    for give in gives[middle - 1 :]:
         give.start()
-    answer = products[:padded]
-    for offset, give in enumerate(gives, 1):
-        give.wait_recv()
+    result = products(0, middle)
+    outgoing[:middle] = result.reshape(middle, padded, 2 * out_width).astype(BF16)
+    for give in gives[: middle - 1]:
+        give.start()
+    answer = result[:padded]
+    for offset in list(range(middle, peers)) + list(range(1, middle)):
+        gives[offset - 1].wait_recv()
         answer = answer + incoming[offset].astype(F32)
     answer = answer.astype(out_ref.dtype)
     out_ref[0, 0] = answer[:count, :out_width]
     out_ref[1, 0] = answer[:count, out_width:]
-    for give in gives:
-        give.wait_send()
+    for copy in asks + gives:
+        copy.wait_send()
 
 
 def fused(mode_size, group_size, padded, arguments):
@@ -287,10 +313,10 @@
             pltpu.VMEM(mode_labels.shape, jnp.int32),
             pltpu.VMEM(requests.shape, jnp.int32),
             pltpu.VMEM((peers, width), jnp.int32),
-            pltpu.VMEM((terms, row_count // sub, width), F32),
-            pltpu.VMEM((terms, total, width), F32),
-            pltpu.VMEM((2 * fold, total, span), F32),
-            pltpu.VMEM((2 * fold, total, width), F32),
+            pltpu.VMEM((terms, row_count // sub, width), BF16),
+            pltpu.VMEM((total // TILE, span, width), BF16),
+            pltpu.VMEM((total // TILE, 2 * fold * TILE, span), BF16),
+            pltpu.VMEM((2 * fold, total, width), BF16),
             pltpu.VMEM((peers, padded, 2 * out_width), BF16),
             pltpu.VMEM((peers, padded, 2 * out_width), BF16),
             dma((7,)),

time: 20.1 us -> 19.3 us (0.960)
  Pallas kernels: 18.5 us -> 17.7 us
    pallas_call x1, Pallas kernels: 18.5 us -> 17.7 us  [fused(): pl.pallas_call(functools.partial(fused_kernel, mode_size, group_size), ou...]
where the time goes in v3:
time: 19.3 us; the launch traced here: 19 us
  Pallas kernels  17.7 us (92%)
  local copies, waits for them, and re-layouts  1.33 us (7%)
    pallas_call x1, Pallas kernels, fused(): pl.pallas_call(functools.partial(fused_kernel, mode_size, group_size), ou...  17.7 us
    pallas_call x1, local copies, waits for them, and re-layouts, fused(): pl.pallas_call(functools.partial(fused_kernel, mode_size, group_size), ou...  1.33 us

profile of v3, /device:TPU:0, one launch (start us, length us, event | category | flops | bytes accessed | tf_op | source)
XLA Modules:
  0.0 19.0 jit_solution(5646354437355078149)
XLA Ops:
  0.0 17.7 %shard_map.82 = bf16[2,1,29,128]{3,2,1,0:T(8,128)(2,1)} custom-call(bf16[2,1,2048,128]{3,2,1,0:T(8,128)(2,1)} %stem_hbm.1, bf16[2,128,128]{2,1,0:T(8,128)(2,1)} %column_hbm.1, bf16[2,128,128]{2,1,0:T(8,128)(2,1)} %row_hbm.1, bf16[2,128,128]{2,1,0:T(8,128)(2,1)} %mode_hbm.1, bf16[2,1024,128]{2,1,0:T(8,128)(2,1)} %final_hbm.1, s32[1,128]{1,0:T(1,128)} %bitcast.2, ...), custom_call_target="tpu_custom_call" | custom-call | tf_op jit(solution)/shard_map/pallas_call | solution.py:301
  17.7 1.3 %copy.9 = bf16[2,1,29,128]{3,0,2,1:T(2,128)(2,1)} copy(bf16[2,1,29,128]{3,2,1,0:T(8,128)(2,1)} %shard_map.82) | data formatting | bytes 29696 | tf_op jit(solution)/shard_map/pallas_call | solution.py:301

commit v4 on v3

--- a/solution.py
+++ b/solution.py
@@ -25,6 +25,18 @@
 
 def iota(shape, dim):
     return lax.broadcasted_iota(jnp.int32, shape, dim)
+
+
+def loop(start, stop, body, unroll=2):
+    def run(trip, carry):
+        for index in range(unroll):
+            body(start + trip * unroll + index)
+        return carry
+
+    trips = (stop - start) // unroll
+    lax.fori_loop(0, trips, run, 0)
+    for step in range(start + trips * unroll, stop):
+        body(step)
 
 
 def complex_rows(real, imag, axis):
@@ -145,7 +157,7 @@
     row_table = jnp.concatenate(complex_rows(row_real, row_imag, 1), 0)
 
     def mix(step):
-        rows = pl.ds(step * step_rows, step_rows)
+        rows = pl.ds(pl.multiple_of(step * step_rows, step_rows), step_rows)
         operand = jnp.concatenate([stem[0, rows, :], stem[1, rows, :]], 1)
         mixed = dot(operand, column_table).astype(BF16)
         pieces = []
@@ -157,12 +169,11 @@
             result[:, index * width : (index + 1) * width].reshape(terms, heads, width)
             for index in range(ROWS_STEP)
         ]
-        first = step * ROWS_STEP * heads
-        spread[:, first : first + ROWS_STEP * heads, :] = jnp.concatenate(result, 1).astype(BF16)
+        found = pl.ds(pl.multiple_of(step * ROWS_STEP * heads, 16), ROWS_STEP * heads)
+        spread[:, found, :] = jnp.concatenate(result, 1).astype(BF16)
 
     steps = groups // ROWS_STEP
-    for step in range(steps // 2):
-        mix(step)
+    loop(0, steps // 2, mix)
 
     pl.semaphore_wait(barrier, peers - 1)
     asks = [
@@ -181,8 +192,7 @@
     for load in small[4:]:
         load.wait()
 
-    for step in range(steps // 2, steps):
-        mix(step)
+    loop(steps // 2, steps, mix)
 
     own = (iota((sub, order), 0) + me * sub == mode_labels[...]).astype(BF16)
     mode_real, mode_imag = dot(own, mode[0]), dot(own, mode[1])
@@ -214,38 +224,50 @@
 
     lane = iota((total, blocks), 1).astype(F32)
     pick = (column_of(block_ids, blocks) == lane).astype(BF16)
-    for term in range(0, terms, 2):
-        found = dot(pick, jnp.concatenate([spread[term], spread[term + 1]], 1))
-        picked[:, term * TILE : (term + 2) * TILE, :] = paired(found[:, :width], found[:, width:])
-
-    order_column = column_of(order_ids, order)
-    lane = iota((total, order), 1).astype(F32)
+
+    def pick_pair(pair):
+        found = dot(pick, jnp.concatenate([spread[2 * pair], spread[2 * pair + 1]], 1))
+        rows = pl.ds(pl.multiple_of(pair * 2 * TILE, 2 * TILE), 2 * TILE)
+        picked[:, rows, :] = paired(found[:, :width], found[:, width:])
+
+    loop(0, terms // 2, pick_pair)
+
+    order_column = column_of(order_ids, order).astype(jnp.int32)
+    lane = iota((total, order), 1)
     same = (iota((TILE, 2 * span), 1) & (TILE - 1)) == iota((TILE, 2 * span), 0)
     same = jnp.broadcast_to(same[None], (tiles, TILE, 2 * span)).reshape(total, 2 * span)
 
     def coefficients(index):
-        at = (order_column + float(index) == lane).astype(BF16)
+        at = (order_column == lane - index).astype(BF16)
         return jnp.where(same, dot_t(at, mode_table), 0.0)
 
-    for index in range(0, fold, 2):
-        first, second = coefficients(index), coefficients(index + 1)
+    def coefficient_pair(pair):
+        first, second = coefficients(2 * pair), coefficients(2 * pair + 1)
         for half in range(2):
-            rows = (half * fold + index) * TILE
+            start = (half * (fold // 2) + pair) * 2 * TILE
+            rows = pl.ds(pl.multiple_of(start, 2 * TILE), 2 * TILE)
             lanes = slice(half * span, (half + 1) * span)
-            coeffs[:, rows : rows + 2 * TILE, :] = paired(first[:, lanes], second[:, lanes])
+            coeffs[:, rows, :] = paired(first[:, lanes], second[:, lanes])
+
+    loop(0, fold // 2, coefficient_pair, 1)
 
     final_real = jnp.concatenate([final[0], final[1]], 1)
     final_imag = jnp.concatenate([-final[1], final[0]], 1)
 
     def products(first_slot, last_slot):
         first, last = first_slot * padded, last_slot * padded
-        for row_start in range(first, last, 2 * TILE):
-            tile = row_start // TILE
+
+        def tile_pair(pair):
             both = [
-                dot(coeffs[tile + index], picked[tile + index]).reshape(2 * fold, TILE, width)
+                dot(coeffs[2 * pair + index], picked[2 * pair + index]).reshape(
+                    2 * fold, TILE, width
+                )
                 for index in range(2)
             ]
-            partial[:, row_start : row_start + 2 * TILE, :] = jnp.concatenate(both, 1).astype(BF16)
+            rows = pl.ds(pl.multiple_of(pair * 2 * TILE, 2 * TILE), 2 * TILE)
+            partial[:, rows, :] = jnp.concatenate(both, 1).astype(BF16)
+
+        loop(first // (2 * TILE), last // (2 * TILE), tile_pair, 4)
         rows = slice(first, last)
         real = jnp.concatenate([partial[index, rows] for index in range(fold)], 1)
         imag = jnp.concatenate([partial[fold + index, rows] for index in range(fold)], 1)
@@ -300,7 +322,7 @@
     dma = pltpu.SemaphoreType.DMA
     return pl.pallas_call(
         functools.partial(fused_kernel, mode_size, group_size),
-        out_shape=jax.ShapeDtypeStruct((2, 1, count, out_width), BF16),
+        out_shape=pltpu.VMEM((2, 1, count, out_width), BF16),
         in_specs=[pl.BlockSpec(memory_space=pltpu.HBM)] * 8,
         out_specs=pl.BlockSpec(memory_space=pltpu.VMEM),
         scratch_shapes=[

time: 19.3 us -> 20.2 us (1.047)
  Pallas kernels: 17.7 us -> 19.4 us
  local copies, waits for them, and re-layouts: 1.33 us -> 0.61 us
    pallas_call x1, Pallas kernels: 17.7 us -> 19.4 us  [fused(): pl.pallas_call(functools.partial(fused_kernel, mode_size, group_size), ou...]
    pallas_call x1, local copies, waits for them, and re-layouts: 1.33 us -> 0.61 us  [fused(): pl.pallas_call(functools.partial(fused_kernel, mode_size, group_size), ou...]
where the time goes in v4:
time: 20.2 us; the launch traced here: 20.1 us
  Pallas kernels  19.4 us (96%)
  local copies, waits for them, and re-layouts  0.61 us (3%)
    pallas_call x1, Pallas kernels, fused(): pl.pallas_call(functools.partial(fused_kernel, mode_size, group_size), ou...  19.4 us
    pallas_call x1, local copies, waits for them, and re-layouts, fused(): pl.pallas_call(functools.partial(fused_kernel, mode_size, group_size), ou...  0.61 us

profile of v4, /device:TPU:0, one launch (start us, length us, event | category | flops | bytes accessed | tf_op | source)
XLA Modules:
  0.0 20.1 jit_solution(17768822823706077035)
XLA Ops:
  0.0 19.4 %shard_map.82 = bf16[2,1,29,128]{3,2,1,0:T(8,128)(2,1)S(1)} custom-call(bf16[2,1,2048,128]{3,2,1,0:T(8,128)(2,1)} %stem_hbm.1, bf16[2,128,128]{2,1,0:T(8,128)(2,1)} %column_hbm.1, bf16[2,128,128]{2,1,0:T(8,128)(2,1)} %row_hbm.1, bf16[2,128,128]{2,1,0:T(8,128)(2,1)} %mode_hbm.1, bf16[2,1024,128]{2,1,0:T(8,128)(2,1)} %final_hbm.1, s32[1,128]{1,0:T(1,128)} %bitcast.2, ...), custom_call_target="tpu_custom_call" | custom-call | tf_op jit(solution)/shard_map/pallas_call | solution.py:323
  19.5 0.6 %copy.9 = bf16[2,1,29,128]{3,0,2,1:T(2,128)(2,1)} copy(bf16[2,1,29,128]{3,2,1,0:T(8,128)(2,1)S(1)} %shard_map.82) | data formatting | bytes 29696 | tf_op jit(solution)/shard_map/pallas_call | solution.py:323

commit v5 on v3

--- a/solution.py
+++ b/solution.py
@@ -300,7 +300,7 @@
     dma = pltpu.SemaphoreType.DMA
     return pl.pallas_call(
         functools.partial(fused_kernel, mode_size, group_size),
-        out_shape=jax.ShapeDtypeStruct((2, 1, count, out_width), BF16),
+        out_shape=pltpu.VMEM((2, 1, count, out_width), BF16),
         in_specs=[pl.BlockSpec(memory_space=pltpu.HBM)] * 8,
         out_specs=pl.BlockSpec(memory_space=pltpu.VMEM),
         scratch_shapes=[

time: 19.3 us -> 17.9 us (0.927)
  local copies, waits for them, and re-layouts: 1.33 us -> 0.61 us
  Pallas kernels: 17.7 us -> 17.1 us
    pallas_call x1, local copies, waits for them, and re-layouts: 1.33 us -> 0.61 us  [fused(): pl.pallas_call(functools.partial(fused_kernel, mode_size, group_size), ou...]
    pallas_call x1, Pallas kernels: 17.7 us -> 17.1 us  [fused(): pl.pallas_call(functools.partial(fused_kernel, mode_size, group_size), ou...]
where the time goes in v5:
time: 17.9 us; the launch traced here: 17.7 us
  Pallas kernels  17.1 us (96%)
  local copies, waits for them, and re-layouts  0.61 us (3%)
    pallas_call x1, Pallas kernels, fused(): pl.pallas_call(functools.partial(fused_kernel, mode_size, group_size), ou...  17.1 us
    pallas_call x1, local copies, waits for them, and re-layouts, fused(): pl.pallas_call(functools.partial(fused_kernel, mode_size, group_size), ou...  0.61 us

profile of v5, /device:TPU:0, one launch (start us, length us, event | category | flops | bytes accessed | tf_op | source)
XLA Modules:
  0.0 17.7 jit_solution(15488630661325840966)
XLA Ops:
  0.0 17.1 %shard_map.82 = bf16[2,1,29,128]{3,2,1,0:T(8,128)(2,1)S(1)} custom-call(bf16[2,1,2048,128]{3,2,1,0:T(8,128)(2,1)} %stem_hbm.1, bf16[2,128,128]{2,1,0:T(8,128)(2,1)} %column_hbm.1, bf16[2,128,128]{2,1,0:T(8,128)(2,1)} %row_hbm.1, bf16[2,128,128]{2,1,0:T(8,128)(2,1)} %mode_hbm.1, bf16[2,1024,128]{2,1,0:T(8,128)(2,1)} %final_hbm.1, s32[1,128]{1,0:T(1,128)} %bitcast.2, ...), custom_call_target="tpu_custom_call" | custom-call | tf_op jit(solution)/shard_map/pallas_call | solution.py:301
  17.1 0.6 %copy.9 = bf16[2,1,29,128]{3,0,2,1:T(2,128)(2,1)} copy(bf16[2,1,29,128]{3,2,1,0:T(8,128)(2,1)S(1)} %shard_map.82) | data formatting | bytes 29696 | tf_op jit(solution)/shard_map/pallas_call | solution.py:301

commit v6 on v5

--- a/solution.py
+++ b/solution.py
@@ -77,19 +77,22 @@
     out_width = final.shape[2]
     count = wanted.shape[1]
     padded = outgoing.shape[1]
-    total = peers * padded
     blocks = row_count // sub
     row_blocks = order // fold
     terms = 2 * sub
     span = terms * TILE
-    tiles = total // TILE
 
     mode_index = lax.axis_index("mode")
     group_index = lax.axis_index("group")
     me = mode_index * group_size + group_index
 
     def device(offset):
-        peer = lax.rem(me + offset, peers)
+        peer = me
+        bit = 1
+        while bit <= offset:
+            if offset & bit:
+                peer = peer + bit - 2 * bit * lax.rem(peer // bit, 2)
+            bit *= 2
         return {"mode": peer // group_size, "group": lax.rem(peer, group_size)}
 
     barrier = pltpu.get_barrier_semaphore()
@@ -188,9 +191,7 @@
     mode_real, mode_imag = dot(own, mode[0]), dot(own, mode[1])
     cube = (terms, TILE, terms)
     repeat = (iota(cube, 0) == iota(cube, 2)).astype(F32).reshape(span, terms).astype(BF16)
-    mode_table = jnp.concatenate(
-        [dot(repeat, half.astype(BF16)) for half in complex_rows(mode_real, mode_imag, 0)], 0
-    ).astype(BF16)
+    mode_table = dot(repeat, jnp.concatenate([mode_real, mode_imag], 0).astype(BF16)).astype(BF16)
 
     for ask in asks:
         ask.wait_recv()
@@ -198,47 +199,54 @@
     block_ids = jnp.transpose(lax.div(ids, row_blocks).astype(F32))
     order_ids = jnp.transpose((lax.rem(ids, row_blocks) * fold).astype(F32))
 
-    def column_of(values, lanes):
-        return jnp.concatenate(
-            [
-                jnp.broadcast_to(values[:padded, slot : slot + 1], (padded, lanes))
-                for slot in range(peers)
-            ],
-            0,
-        )
-
-    def paired(first, second):
-        lanes = first.shape[1]
-        both = [part.reshape(tiles, TILE, lanes) for part in (first, second)]
-        return jnp.concatenate(both, 1).astype(BF16)
-
-    lane = iota((total, blocks), 1).astype(F32)
-    pick = (column_of(block_ids, blocks) == lane).astype(BF16)
-    for term in range(0, terms, 2):
-        found = dot(pick, jnp.concatenate([spread[term], spread[term + 1]], 1))
-        picked[:, term * TILE : (term + 2) * TILE, :] = paired(found[:, :width], found[:, width:])
-
-    order_column = column_of(order_ids, order)
-    lane = iota((total, order), 1).astype(F32)
-    same = (iota((TILE, 2 * span), 1) & (TILE - 1)) == iota((TILE, 2 * span), 0)
-    same = jnp.broadcast_to(same[None], (tiles, TILE, 2 * span)).reshape(total, 2 * span)
-
-    def coefficients(index):
-        at = (order_column + float(index) == lane).astype(BF16)
-        return jnp.where(same, dot_t(at, mode_table), 0.0)
-
-    for index in range(0, fold, 2):
-        first, second = coefficients(index), coefficients(index + 1)
-        for half in range(2):
-            rows = (half * fold + index) * TILE
-            lanes = slice(half * span, (half + 1) * span)
-            coeffs[:, rows : rows + 2 * TILE, :] = paired(first[:, lanes], second[:, lanes])
-
     final_real = jnp.concatenate([final[0], final[1]], 1)
     final_imag = jnp.concatenate([-final[1], final[0]], 1)
 
     def products(first_slot, last_slot):
         first, last = first_slot * padded, last_slot * padded
+        rows = last - first
+        tiles = rows // TILE
+        first_tile = first // TILE
+
+        def column_of(values, lanes):
+            return jnp.concatenate(
+                [
+                    jnp.broadcast_to(values[:padded, slot : slot + 1], (padded, lanes))
+                    for slot in range(first_slot, last_slot)
+                ],
+                0,
+            )
+
+        def paired(one, other):
+            lanes = one.shape[1]
+            both = [part.reshape(tiles, TILE, lanes) for part in (one, other)]
+            return jnp.concatenate(both, 1).astype(BF16)
+
+        pick = (column_of(block_ids, blocks) == iota((rows, blocks), 1).astype(F32)).astype(BF16)
+        for term in range(0, terms, 2):
+            found = dot(pick, jnp.concatenate([spread[term], spread[term + 1]], 1))
+            picked[first_tile : first_tile + tiles, term * TILE : (term + 2) * TILE, :] = paired(
+                found[:, :width], found[:, width:]
+            )
+
+        order_column = column_of(order_ids, order)
+        lane = iota((rows, order), 1).astype(F32)
+        same = (iota((TILE, span), 1) & (TILE - 1)) == iota((TILE, span), 0)
+        same = jnp.broadcast_to(same[None], (tiles, TILE, span)).reshape(rows, span)
+
+        def coefficients(index):
+            at = (order_column + float(index) == lane).astype(BF16)
+            return jnp.where(same, dot_t(at, mode_table), 0.0)
+
+        for index in range(0, fold, 2):
+            pair = paired(coefficients(index), coefficients(index + 1))
+            real, imag = pair[:, :, : span // 2], pair[:, :, span // 2 :]
+            for half, both in enumerate(((real, -imag), (imag, real))):
+                start = (half * fold + index) * TILE
+                coeffs[
+                    first_tile : first_tile + tiles, start : start + 2 * TILE, :
+                ] = jnp.concatenate(both, 2)
+
         for row_start in range(first, last, 2 * TILE):
             tile = row_start // TILE
             both = [
@@ -246,9 +254,8 @@
                 for index in range(2)
             ]
             partial[:, row_start : row_start + 2 * TILE, :] = jnp.concatenate(both, 1).astype(BF16)
-        rows = slice(first, last)
-        real = jnp.concatenate([partial[index, rows] for index in range(fold)], 1)
-        imag = jnp.concatenate([partial[fold + index, rows] for index in range(fold)], 1)
+        real = jnp.concatenate([partial[index, first:last] for index in range(fold)], 1)
+        imag = jnp.concatenate([partial[fold + index, first:last] for index in range(fold)], 1)
         return dot(real, final_real) + dot(imag, final_imag)
 
     gives = [
@@ -257,7 +264,7 @@
             dst_ref=incoming.at[offset],
             send_sem=give_send.at[offset],
             recv_sem=give_recv.at[offset],
-            device_id=device(peers - offset),
+            device_id=device(offset),
             device_id_type=pl.DeviceIdType.MESH,
         )
         for offset in range(1, peers)

time: 17.9 us -> 17.1 us (0.955)
  Pallas kernels: 17.1 us -> 16.3 us
    pallas_call x1, Pallas kernels: 17.1 us -> 16.3 us  [fused(): pl.pallas_call(functools.partial(fused_kernel, mode_size, group_size), ou...]
where the time goes in v6:
time: 17.1 us; the launch traced here: 17 us
  Pallas kernels  16.3 us (95%)
  local copies, waits for them, and re-layouts  0.61 us (4%)
    pallas_call x1, Pallas kernels, fused(): pl.pallas_call(functools.partial(fused_kernel, mode_size, group_size), ou...  16.3 us
    pallas_call x1, local copies, waits for them, and re-layouts, fused(): pl.pallas_call(functools.partial(fused_kernel, mode_size, group_size), ou...  0.61 us

profile of v6, /device:TPU:0, one launch (start us, length us, event | category | flops | bytes accessed | tf_op | source)
XLA Modules:
  0.0 17.0 jit_solution(11622844928721607984)
XLA Ops:
  0.0 16.3 %shard_map.82 = bf16[2,1,29,128]{3,2,1,0:T(8,128)(2,1)S(1)} custom-call(bf16[2,1,2048,128]{3,2,1,0:T(8,128)(2,1)} %stem_hbm.1, bf16[2,128,128]{2,1,0:T(8,128)(2,1)} %column_hbm.1, bf16[2,128,128]{2,1,0:T(8,128)(2,1)} %row_hbm.1, bf16[2,128,128]{2,1,0:T(8,128)(2,1)} %mode_hbm.1, bf16[2,1024,128]{2,1,0:T(8,128)(2,1)} %final_hbm.1, s32[1,128]{1,0:T(1,128)} %bitcast.2, ...), custom_call_target="tpu_custom_call" | custom-call | tf_op jit(solution)/shard_map/pallas_call | solution.py:308
  16.4 0.6 %copy.9 = bf16[2,1,29,128]{3,0,2,1:T(2,128)(2,1)} copy(bf16[2,1,29,128]{3,2,1,0:T(8,128)(2,1)S(1)} %shard_map.82) | data formatting | bytes 29696 | tf_op jit(solution)/shard_map/pallas_call | solution.py:308

commit v7 on v6

--- a/solution.py
+++ b/solution.py
@@ -20,7 +20,7 @@
 
 
 def dot_t(left, right):
-    return lax.dot_general(left, right, (((1,), (1,)), ((), ())), preferred_element_type=F32)
+    return lax.dot_general(left, right, (((0,), (1,)), ((), ())), preferred_element_type=F32)
 
 
 def iota(shape, dim):
@@ -52,13 +52,14 @@
     mode_labels,
     wanted,
     asked,
+    indices,
     spread,
-    picked,
     coeffs,
     partial,
     outgoing,
     incoming,
     load_sem,
+    index_sem,
     stem_sem,
     ask_send,
     ask_recv,
@@ -128,24 +129,40 @@
         load.start()
 
     small[0].wait()
-    asked[0:1, :] = jnp.zeros((1, width), jnp.int32)
-    asked[0:1, 0:count] = wanted[...]
-    for load in small[1:4] + stem_loads:
+    asked[0:2, :] = jnp.zeros((2, width), jnp.int32)
+    asked[0:1, 0:count] = lax.div(wanted[...], row_blocks)
+    asked[1:2, 0:count] = lax.rem(wanted[...], row_blocks)
+    pl.semaphore_wait(barrier, peers - 1)
+    asks = [
+        pltpu.make_async_remote_copy(
+            src_ref=asked.at[pl.ds(0, 2), :],
+            dst_ref=asked.at[pl.ds(2 * offset, 2), :],
+            send_sem=ask_send.at[offset],
+            recv_sem=ask_recv.at[offset],
+            device_id=device(offset),
+            device_id_type=pl.DeviceIdType.MESH,
+        )
+        for offset in range(1, peers)
+    ]
+    for ask in asks:
+        ask.start()
+    for load in small[1:] + stem_loads:
         load.wait()
 
     column_real, column_imag = complex_rows(column[0], column[1], 0)
     column_table = jnp.concatenate([column_real, column_imag], 1)
     chosen = (iota((row_order, row_order), 0) == row_labels[...]).astype(BF16)
-    cube = (sub, heads, row_order)
-    swap_rows = (
-        (iota(cube, 1) * sub + iota(cube, 0) == iota(cube, 2))
-        .astype(F32)
-        .reshape(row_order, row_order)
-        .astype(BF16)
-    )
-    row_real = dot_t(swap_rows, dot(chosen, row[0]).astype(BF16)).astype(BF16)
-    row_imag = dot_t(swap_rows, dot(chosen, row[1]).astype(BF16)).astype(BF16)
-    row_table = jnp.concatenate(complex_rows(row_real, row_imag, 1), 0)
+
+    def relabelled(weight):
+        return dot_t(weight, chosen).astype(BF16)
+
+    row_table = jnp.concatenate(
+        [
+            half.reshape(heads, sub, 2 * row_order)
+            for half in complex_rows(relabelled(row[0]), relabelled(row[1]), 1)
+        ],
+        1,
+    ).reshape(2 * row_order, 2 * row_order)
 
     def mix(step):
         rows = pl.ds(step * step_rows, step_rows)
@@ -156,106 +173,63 @@
             piece = mixed[index * row_order : (index + 1) * row_order]
             pieces.append(jnp.concatenate([piece[:, :width], piece[:, width:]], 0))
         result = dot(row_table, jnp.concatenate(pieces, 1))
-        result = [
-            result[:, index * width : (index + 1) * width].reshape(terms, heads, width)
-            for index in range(ROWS_STEP)
-        ]
-        first = step * ROWS_STEP * heads
-        spread[:, first : first + ROWS_STEP * heads, :] = jnp.concatenate(result, 1).astype(BF16)
-
-    steps = groups // ROWS_STEP
-    for step in range(steps // 2):
-        mix(step)
-
-    pl.semaphore_wait(barrier, peers - 1)
-    asks = [
-        pltpu.make_async_remote_copy(
-            src_ref=asked.at[pl.ds(0, 1), :],
-            dst_ref=asked.at[pl.ds(offset, 1), :],
-            send_sem=ask_send.at[offset],
-            recv_sem=ask_recv.at[offset],
-            device_id=device(offset),
-            device_id_type=pl.DeviceIdType.MESH,
-        )
-        for offset in range(1, peers)
-    ]
-    for ask in asks:
-        ask.start()
-    for load in small[4:]:
-        load.wait()
-
-    for step in range(steps // 2, steps):
+        for index in range(ROWS_STEP):
+            first = (step * ROWS_STEP + index) * heads
+            spread[first : first + heads] = (
+                result[:, index * width : (index + 1) * width]
+                .reshape(heads, terms, width)
+                .astype(BF16)
+            )
+
+    for step in range(groups // ROWS_STEP):
         mix(step)
 
     own = (iota((sub, order), 0) + me * sub == mode_labels[...]).astype(BF16)
     mode_real, mode_imag = dot(own, mode[0]), dot(own, mode[1])
-    cube = (terms, TILE, terms)
-    repeat = (iota(cube, 0) == iota(cube, 2)).astype(F32).reshape(span, terms).astype(BF16)
-    mode_table = dot(repeat, jnp.concatenate([mode_real, mode_imag], 0).astype(BF16)).astype(BF16)
+    lane = iota((terms, span), 1)
+    repeat = functools.reduce(
+        jnp.logical_or,
+        [lane == iota((terms, span), 0) + place * terms for place in range(TILE)],
+    ).astype(BF16)
+    blocks_of = jnp.concatenate(
+        [
+            dot(jnp.transpose(half).astype(BF16), repeat).reshape(row_blocks, fold, span)
+            for half in complex_rows(mode_real, mode_imag, 0)
+        ],
+        1,
+    )
+    lane = iota(blocks_of.shape, 2)
+    for place in range(TILE):
+        inside = (lane >= place * terms) & (lane < (place + 1) * terms)
+        coeffs[place] = jnp.where(inside, blocks_of, 0.0).astype(BF16)
+
+    final_real = jnp.concatenate([final[0], final[1]], 1)
+    final_imag = jnp.concatenate([-final[1], final[0]], 1)
 
     for ask in asks:
         ask.wait_recv()
-    ids = asked[...]
-    block_ids = jnp.transpose(lax.div(ids, row_blocks).astype(F32))
-    order_ids = jnp.transpose((lax.rem(ids, row_blocks) * fold).astype(F32))
-
-    final_real = jnp.concatenate([final[0], final[1]], 1)
-    final_imag = jnp.concatenate([-final[1], final[0]], 1)
+    to_scalars = pltpu.make_async_copy(asked, indices, index_sem)
+    to_scalars.start()
+    to_scalars.wait()
 
     def products(first_slot, last_slot):
         first, last = first_slot * padded, last_slot * padded
         rows = last - first
-        tiles = rows // TILE
-        first_tile = first // TILE
-
-        def column_of(values, lanes):
-            return jnp.concatenate(
-                [
-                    jnp.broadcast_to(values[:padded, slot : slot + 1], (padded, lanes))
-                    for slot in range(first_slot, last_slot)
-                ],
-                0,
+        for start in range(first, last, TILE):
+            left, right = [], []
+            for place in range(TILE):
+                slot, entry = (start + place) // padded, (start + place) % padded
+                left.append(coeffs[place, indices[2 * slot + 1, entry]])
+                right.append(spread[indices[2 * slot, entry]])
+            partial[start * 2 * fold : (start + TILE) * 2 * fold, :] = dot(
+                jnp.concatenate(left, 0), jnp.concatenate(right, 0)
             )
-
-        def paired(one, other):
-            lanes = one.shape[1]
-            both = [part.reshape(tiles, TILE, lanes) for part in (one, other)]
-            return jnp.concatenate(both, 1).astype(BF16)
-
-        pick = (column_of(block_ids, blocks) == iota((rows, blocks), 1).astype(F32)).astype(BF16)
-        for term in range(0, terms, 2):
-            found = dot(pick, jnp.concatenate([spread[term], spread[term + 1]], 1))
-            picked[first_tile : first_tile + tiles, term * TILE : (term + 2) * TILE, :] = paired(
-                found[:, :width], found[:, width:]
-            )
-
-        order_column = column_of(order_ids, order)
-        lane = iota((rows, order), 1).astype(F32)
-        same = (iota((TILE, span), 1) & (TILE - 1)) == iota((TILE, span), 0)
-        same = jnp.broadcast_to(same[None], (tiles, TILE, span)).reshape(rows, span)
-
-        def coefficients(index):
-            at = (order_column + float(index) == lane).astype(BF16)
-            return jnp.where(same, dot_t(at, mode_table), 0.0)
-
-        for index in range(0, fold, 2):
-            pair = paired(coefficients(index), coefficients(index + 1))
-            real, imag = pair[:, :, : span // 2], pair[:, :, span // 2 :]
-            for half, both in enumerate(((real, -imag), (imag, real))):
-                start = (half * fold + index) * TILE
-                coeffs[
-                    first_tile : first_tile + tiles, start : start + 2 * TILE, :
-                ] = jnp.concatenate(both, 2)
-
-        for row_start in range(first, last, 2 * TILE):
-            tile = row_start // TILE
-            both = [
-                dot(coeffs[tile + index], picked[tile + index]).reshape(2 * fold, TILE, width)
-                for index in range(2)
-            ]
-            partial[:, row_start : row_start + 2 * TILE, :] = jnp.concatenate(both, 1).astype(BF16)
-        real = jnp.concatenate([partial[index, first:last] for index in range(fold)], 1)
-        imag = jnp.concatenate([partial[fold + index, first:last] for index in range(fold)], 1)
+        pieces = [
+            partial[pl.ds(first * 2 * fold + index, rows, stride=2 * fold), :].astype(BF16)
+            for index in range(2 * fold)
+        ]
+        real = jnp.concatenate(pieces[:fold], 1)
+        imag = jnp.concatenate(pieces[fold:], 1)
         return dot(real, final_real) + dot(imag, final_imag)
 
     gives = [
@@ -319,14 +293,15 @@
             pltpu.VMEM(row_labels.shape, jnp.int32),
             pltpu.VMEM(mode_labels.shape, jnp.int32),
             pltpu.VMEM(requests.shape, jnp.int32),
-            pltpu.VMEM((peers, width), jnp.int32),
-            pltpu.VMEM((terms, row_count // sub, width), BF16),
-            pltpu.VMEM((total // TILE, span, width), BF16),
-            pltpu.VMEM((total // TILE, 2 * fold * TILE, span), BF16),
-            pltpu.VMEM((2 * fold, total, width), BF16),
+            pltpu.VMEM((2 * peers, width), jnp.int32),
+            pltpu.SMEM((2 * peers, width), jnp.int32),
+            pltpu.VMEM((row_count // sub, terms, width), BF16),
+            pltpu.VMEM((TILE, order // fold, 2 * fold, span), BF16),
+            pltpu.VMEM((total * 2 * fold, width), F32),
             pltpu.VMEM((peers, padded, 2 * out_width), BF16),
             pltpu.VMEM((peers, padded, 2 * out_width), BF16),
             dma((7,)),
+            dma,
             dma((steps,)),
             dma((peers,)),
             dma((peers,)),

time: 17.1 us -> 17.3 us (1.012)
  Pallas kernels: 16.3 us -> 16.5 us
where the time goes in v7:
time: 17.3 us; the launch traced here: 17.1 us
  Pallas kernels  16.5 us (95%)
  local copies, waits for them, and re-layouts  0.61 us (4%)
    pallas_call x1, Pallas kernels, fused(): pl.pallas_call(functools.partial(fused_kernel, mode_size, group_size), ou...  16.5 us
    pallas_call x1, local copies, waits for them, and re-layouts, fused(): pl.pallas_call(functools.partial(fused_kernel, mode_size, group_size), ou...  0.61 us

profile of v7, /device:TPU:0, one launch (start us, length us, event | category | flops | bytes accessed | tf_op | source)
XLA Modules:
  0.0 17.1 jit_solution(8237017242648604606)
XLA Ops:
  0.0 16.5 %shard_map.82 = bf16[2,1,29,128]{3,2,1,0:T(8,128)(2,1)S(1)} custom-call(bf16[2,1,2048,128]{3,2,1,0:T(8,128)(2,1)} %stem_hbm.1, bf16[2,128,128]{2,1,0:T(8,128)(2,1)} %column_hbm.1, bf16[2,128,128]{2,1,0:T(8,128)(2,1)} %row_hbm.1, bf16[2,128,128]{2,1,0:T(8,128)(2,1)} %mode_hbm.1, bf16[2,1024,128]{2,1,0:T(8,128)(2,1)} %final_hbm.1, s32[1,128]{1,0:T(1,128)} %bitcast.2, ...), custom_call_target="tpu_custom_call" | custom-call | tf_op jit(solution)/shard_map/pallas_call | solution.py:282
  16.5 0.6 %copy.9 = bf16[2,1,29,128]{3,0,2,1:T(2,128)(2,1)} copy(bf16[2,1,29,128]{3,2,1,0:T(8,128)(2,1)S(1)} %shard_map.82) | data formatting | bytes 29696 | tf_op jit(solution)/shard_map/pallas_call | solution.py:282

commit v8 on v7

--- a/solution.py
+++ b/solution.py
@@ -132,21 +132,7 @@
     asked[0:2, :] = jnp.zeros((2, width), jnp.int32)
     asked[0:1, 0:count] = lax.div(wanted[...], row_blocks)
     asked[1:2, 0:count] = lax.rem(wanted[...], row_blocks)
-    pl.semaphore_wait(barrier, peers - 1)
-    asks = [
-        pltpu.make_async_remote_copy(
-            src_ref=asked.at[pl.ds(0, 2), :],
-            dst_ref=asked.at[pl.ds(2 * offset, 2), :],
-            send_sem=ask_send.at[offset],
-            recv_sem=ask_recv.at[offset],
-            device_id=device(offset),
-            device_id_type=pl.DeviceIdType.MESH,
-        )
-        for offset in range(1, peers)
-    ]
-    for ask in asks:
-        ask.start()
-    for load in small[1:] + stem_loads:
+    for load in small[1:4] + stem_loads:
         load.wait()
 
     column_real, column_imag = complex_rows(column[0], column[1], 0)
@@ -181,7 +167,27 @@
                 .astype(BF16)
             )
 
-    for step in range(groups // ROWS_STEP):
+    steps = groups // ROWS_STEP
+    for step in range(steps // 2):
+        mix(step)
+
+    pl.semaphore_wait(barrier, peers - 1)
+    asks = [
+        pltpu.make_async_remote_copy(
+            src_ref=asked.at[pl.ds(0, 2), :],
+            dst_ref=asked.at[pl.ds(2 * offset, 2), :],
+            send_sem=ask_send.at[offset],
+            recv_sem=ask_recv.at[offset],
+            device_id=device(offset),
+            device_id_type=pl.DeviceIdType.MESH,
+        )
+        for offset in range(1, peers)
+    ]
+    for ask in asks:
+        ask.start()
+    for load in small[4:]:
+        load.wait()
+    for step in range(steps // 2, steps):
         mix(step)
 
     own = (iota((sub, order), 0) + me * sub == mode_labels[...]).astype(BF16)

time: 17.3 us -> 17.3 us (level)
  no operation moved by 1% of the time
where the time goes in v8:
time: 17.3 us; the launch traced here: 17.1 us
  Pallas kernels  16.5 us (95%)
  local copies, waits for them, and re-layouts  0.61 us (4%)
    pallas_call x1, Pallas kernels, fused(): pl.pallas_call(functools.partial(fused_kernel, mode_size, group_size), ou...  16.5 us
    pallas_call x1, local copies, waits for them, and re-layouts, fused(): pl.pallas_call(functools.partial(fused_kernel, mode_size, group_size), ou...  0.61 us

profile of v8, /device:TPU:0, one launch (start us, length us, event | category | flops | bytes accessed | tf_op | source)
XLA Modules:
  0.0 17.1 jit_solution(18074311789612878394)
XLA Ops:
  0.0 16.5 %shard_map.82 = bf16[2,1,29,128]{3,2,1,0:T(8,128)(2,1)S(1)} custom-call(bf16[2,1,2048,128]{3,2,1,0:T(8,128)(2,1)} %stem_hbm.1, bf16[2,128,128]{2,1,0:T(8,128)(2,1)} %column_hbm.1, bf16[2,128,128]{2,1,0:T(8,128)(2,1)} %row_hbm.1, bf16[2,128,128]{2,1,0:T(8,128)(2,1)} %mode_hbm.1, bf16[2,1024,128]{2,1,0:T(8,128)(2,1)} %final_hbm.1, s32[1,128]{1,0:T(1,128)} %bitcast.2, ...), custom_call_target="tpu_custom_call" | custom-call | tf_op jit(solution)/shard_map/pallas_call | solution.py:288
  16.5 0.6 %copy.9 = bf16[2,1,29,128]{3,0,2,1:T(2,128)(2,1)} copy(bf16[2,1,29,128]{3,2,1,0:T(8,128)(2,1)S(1)} %shard_map.82) | data formatting | bytes 29696 | tf_op jit(solution)/shard_map/pallas_call | solution.py:288

commit v9 on v7

--- a/solution.py
+++ b/solution.py
@@ -9,6 +9,7 @@
 
 CAPACITY = 8
 TILE = 8
+CHUNK_SLOTS = 2
 ROWS_STEP = 2
 
 F32 = jnp.float32
@@ -132,6 +133,24 @@
     asked[0:2, :] = jnp.zeros((2, width), jnp.int32)
     asked[0:1, 0:count] = lax.div(wanted[...], row_blocks)
     asked[1:2, 0:count] = lax.rem(wanted[...], row_blocks)
+    for load in small[1:4]:
+        load.wait()
+
+    column_real, column_imag = complex_rows(column[0], column[1], 0)
+    column_table = jnp.concatenate([column_real, column_imag], 1)
+    chosen = (iota((row_order, row_order), 0) == row_labels[...]).astype(BF16)
+
+    def relabelled(weight):
+        return dot_t(weight, chosen).astype(BF16)
+
+    row_table = jnp.concatenate(
+        [
+            half.reshape(heads, sub, 2 * row_order)
+            for half in complex_rows(relabelled(row[0]), relabelled(row[1]), 1)
+        ],
+        1,
+    ).reshape(2 * row_order, 2 * row_order)
+
     pl.semaphore_wait(barrier, peers - 1)
     asks = [
         pltpu.make_async_remote_copy(
@@ -146,23 +165,8 @@
     ]
     for ask in asks:
         ask.start()
-    for load in small[1:] + stem_loads:
+    for load in stem_loads + small[4:]:
         load.wait()
-
-    column_real, column_imag = complex_rows(column[0], column[1], 0)
-    column_table = jnp.concatenate([column_real, column_imag], 1)
-    chosen = (iota((row_order, row_order), 0) == row_labels[...]).astype(BF16)
-
-    def relabelled(weight):
-        return dot_t(weight, chosen).astype(BF16)
-
-    row_table = jnp.concatenate(
-        [
-            half.reshape(heads, sub, 2 * row_order)
-            for half in complex_rows(relabelled(row[0]), relabelled(row[1]), 1)
-        ],
-        1,
-    ).reshape(2 * row_order, 2 * row_order)
 
     def mix(step):
         rows = pl.ds(step * step_rows, step_rows)
@@ -206,11 +210,14 @@
     final_real = jnp.concatenate([final[0], final[1]], 1)
     final_imag = jnp.concatenate([-final[1], final[0]], 1)
 
-    for ask in asks:
-        ask.wait_recv()
-    to_scalars = pltpu.make_async_copy(asked, indices, index_sem)
-    to_scalars.start()
-    to_scalars.wait()
+    def bring(chunk):
+        first_slot = chunk * CHUNK_SLOTS
+        for slot in range(max(first_slot, 1), first_slot + CHUNK_SLOTS):
+            asks[slot - 1].wait_recv()
+        rows = pl.ds(2 * first_slot, 2 * CHUNK_SLOTS)
+        copy = pltpu.make_async_copy(asked.at[rows, :], indices.at[rows, :], index_sem.at[chunk])
+        copy.start()
+        return copy
 
     def products(first_slot, last_slot):
         first, last = first_slot * padded, last_slot * padded
@@ -243,17 +250,20 @@
         )
         for offset in range(1, peers)
     ]
-    middle = peers // 2
-    result = products(middle, peers)
-    outgoing[middle:] = result.reshape(peers - middle, padded, 2 * out_width).astype(BF16)
-    for give in gives[middle - 1 :]:
-        give.start()
-    result = products(0, middle)
-    outgoing[:middle] = result.reshape(middle, padded, 2 * out_width).astype(BF16)
-    for give in gives[: middle - 1]:
-        give.start()
+    chunks = peers // CHUNK_SLOTS
+    ready = bring(chunks - 1)
+    for chunk in reversed(range(chunks)):
+        ready.wait()
+        if chunk:
+            ready = bring(chunk - 1)
+        first = chunk * CHUNK_SLOTS
+        last = first + CHUNK_SLOTS
+        result = products(first, last)
+        outgoing[first:last] = result.reshape(CHUNK_SLOTS, padded, 2 * out_width).astype(BF16)
+        for give in gives[max(first, 1) - 1 : last - 1]:
+            give.start()
     answer = result[:padded]
-    for offset in list(range(middle, peers)) + list(range(1, middle)):
+    for offset in reversed(range(1, peers)):
         gives[offset - 1].wait_recv()
         answer = answer + incoming[offset].astype(F32)
     answer = answer.astype(out_ref.dtype)
@@ -301,7 +311,7 @@
             pltpu.VMEM((peers, padded, 2 * out_width), BF16),
             pltpu.VMEM((peers, padded, 2 * out_width), BF16),
             dma((7,)),
-            dma,
+            dma((peers // CHUNK_SLOTS,)),
             dma((steps,)),
             dma((peers,)),
             dma((peers,)),

time: 17.3 us -> 16.7 us (0.965)
  Pallas kernels: 16.5 us -> 15.9 us
    pallas_call x1, Pallas kernels: 16.5 us -> 15.9 us  [fused(): pl.pallas_call(functools.partial(fused_kernel, mode_size, group_size), ou...]
where the time goes in v9:
time: 16.7 us; the launch traced here: 16.5 us
  Pallas kernels  15.9 us (95%)
  local copies, waits for them, and re-layouts  0.61 us (4%)
    pallas_call x1, Pallas kernels, fused(): pl.pallas_call(functools.partial(fused_kernel, mode_size, group_size), ou...  15.9 us
    pallas_call x1, local copies, waits for them, and re-layouts, fused(): pl.pallas_call(functools.partial(fused_kernel, mode_size, group_size), ou...  0.61 us

profile of v9, /device:TPU:0, one launch (start us, length us, event | category | flops | bytes accessed | tf_op | source)
XLA Modules:
  0.0 16.5 jit_solution(3250709256942560343)
XLA Ops:
  0.0 15.9 %shard_map.82 = bf16[2,1,29,128]{3,2,1,0:T(8,128)(2,1)S(1)} custom-call(bf16[2,1,2048,128]{3,2,1,0:T(8,128)(2,1)} %stem_hbm.1, bf16[2,128,128]{2,1,0:T(8,128)(2,1)} %column_hbm.1, bf16[2,128,128]{2,1,0:T(8,128)(2,1)} %row_hbm.1, bf16[2,128,128]{2,1,0:T(8,128)(2,1)} %mode_hbm.1, bf16[2,1024,128]{2,1,0:T(8,128)(2,1)} %final_hbm.1, s32[1,128]{1,0:T(1,128)} %bitcast.2, ...), custom_call_target="tpu_custom_call" | custom-call | tf_op jit(solution)/shard_map/pallas_call | solution.py:292
  15.9 0.6 %copy.9 = bf16[2,1,29,128]{3,0,2,1:T(2,128)(2,1)} copy(bf16[2,1,29,128]{3,2,1,0:T(8,128)(2,1)S(1)} %shard_map.82) | data formatting | bytes 29696 | tf_op jit(solution)/shard_map/pallas_call | solution.py:292

commit v10 on v9

--- a/solution.py
+++ b/solution.py
@@ -9,7 +9,6 @@
 
 CAPACITY = 8
 TILE = 8
-CHUNK_SLOTS = 2
 ROWS_STEP = 2
 
 F32 = jnp.float32
@@ -120,11 +119,9 @@
     step_rows = ROWS_STEP * row_order
     stem_loads = [
         pltpu.make_async_copy(
-            stem_hbm.at[:, 0, pl.ds(step * step_rows, step_rows), :],
-            stem.at[:, pl.ds(step * step_rows, step_rows), :],
-            stem_sem.at[step],
+            stem_hbm.at[half, 0], stem.at[half], stem_sem.at[half]
         )
-        for step in range(groups // ROWS_STEP)
+        for half in range(2)
     ]
     for load in small[:4] + stem_loads + small[4:]:
         load.start()
@@ -210,18 +207,14 @@
     final_real = jnp.concatenate([final[0], final[1]], 1)
     final_imag = jnp.concatenate([-final[1], final[0]], 1)
 
-    def bring(chunk):
-        first_slot = chunk * CHUNK_SLOTS
-        for slot in range(max(first_slot, 1), first_slot + CHUNK_SLOTS):
-            asks[slot - 1].wait_recv()
-        rows = pl.ds(2 * first_slot, 2 * CHUNK_SLOTS)
-        copy = pltpu.make_async_copy(asked.at[rows, :], indices.at[rows, :], index_sem.at[chunk])
-        copy.start()
-        return copy
-
-    def products(first_slot, last_slot):
+    for ask in asks:
+        ask.wait_recv()
+    to_scalars = pltpu.make_async_copy(asked, indices, index_sem)
+    to_scalars.start()
+    to_scalars.wait()
+
+    def mode_products(first_slot, last_slot):
         first, last = first_slot * padded, last_slot * padded
-        rows = last - first
         for start in range(first, last, TILE):
             left, right = [], []
             for place in range(TILE):
@@ -231,6 +224,9 @@
             partial[start * 2 * fold : (start + TILE) * 2 * fold, :] = dot(
                 jnp.concatenate(left, 0), jnp.concatenate(right, 0)
             )
+
+    def final_products(first_slot, last_slot):
+        first, rows = first_slot * padded, (last_slot - first_slot) * padded
         pieces = [
             partial[pl.ds(first * 2 * fold + index, rows, stride=2 * fold), :].astype(BF16)
             for index in range(2 * fold)
@@ -250,19 +246,19 @@
         )
         for offset in range(1, peers)
     ]
-    chunks = peers // CHUNK_SLOTS
-    ready = bring(chunks - 1)
-    for chunk in reversed(range(chunks)):
-        ready.wait()
-        if chunk:
-            ready = bring(chunk - 1)
-        first = chunk * CHUNK_SLOTS
-        last = first + CHUNK_SLOTS
-        result = products(first, last)
-        outgoing[first:last] = result.reshape(CHUNK_SLOTS, padded, 2 * out_width).astype(BF16)
-        for give in gives[max(first, 1) - 1 : last - 1]:
-            give.start()
-    answer = result[:padded]
+    middle = peers // 2
+    edges = [peers, middle + middle // 2, middle, 1, 0]
+    chunks = list(zip(edges[1:], edges[:-1]))
+    mode_products(*chunks[0])
+    for index, (first, last) in enumerate(chunks):
+        if index + 1 < len(chunks):
+            mode_products(*chunks[index + 1])
+        result = final_products(first, last)
+        if first:
+            outgoing[first:last] = result.reshape(last - first, padded, 2 * out_width).astype(BF16)
+            for give in gives[first - 1 : last - 1]:
+                give.start()
+    answer = result
     for offset in reversed(range(1, peers)):
         gives[offset - 1].wait_recv()
         answer = answer + incoming[offset].astype(F32)
@@ -285,7 +281,6 @@
     total = peers * padded
     terms = 2 * sub
     span = terms * TILE
-    steps = row_count // row.shape[1] // ROWS_STEP
     row_labels = row_labels.reshape(1, -1)
     mode_labels = mode_labels.reshape(1, -1)
     dma = pltpu.SemaphoreType.DMA
@@ -311,8 +306,8 @@
             pltpu.VMEM((peers, padded, 2 * out_width), BF16),
             pltpu.VMEM((peers, padded, 2 * out_width), BF16),
             dma((7,)),
-            dma((peers // CHUNK_SLOTS,)),
-            dma((steps,)),
+            dma,
+            dma((2,)),
             dma((peers,)),
             dma((peers,)),
             dma((peers,)),

time: 16.7 us -> 16.8 us (level)
  no operation moved by 1% of the time
where the time goes in v10:
time: 16.8 us; the launch traced here: 16.6 us
  Pallas kernels  16 us (95%)
  local copies, waits for them, and re-layouts  0.61 us (4%)
    pallas_call x1, Pallas kernels, fused(): pl.pallas_call(functools.partial(fused_kernel, mode_size, group_size), ou...  16 us
    pallas_call x1, local copies, waits for them, and re-layouts, fused(): pl.pallas_call(functools.partial(fused_kernel, mode_size, group_size), ou...  0.61 us

profile of v10, /device:TPU:0, one launch (start us, length us, event | category | flops | bytes accessed | tf_op | source)
XLA Modules:
  0.0 16.6 jit_solution(13354095808922216815)
XLA Ops:
  0.0 16.0 %shard_map.82 = bf16[2,1,29,128]{3,2,1,0:T(8,128)(2,1)S(1)} custom-call(bf16[2,1,2048,128]{3,2,1,0:T(8,128)(2,1)} %stem_hbm.1, bf16[2,128,128]{2,1,0:T(8,128)(2,1)} %column_hbm.1, bf16[2,128,128]{2,1,0:T(8,128)(2,1)} %row_hbm.1, bf16[2,128,128]{2,1,0:T(8,128)(2,1)} %mode_hbm.1, bf16[2,1024,128]{2,1,0:T(8,128)(2,1)} %final_hbm.1, s32[1,128]{1,0:T(1,128)} %bitcast.2, ...), custom_call_target="tpu_custom_call" | custom-call | tf_op jit(solution)/shard_map/pallas_call | solution.py:287
  16.0 0.6 %copy.9 = bf16[2,1,29,128]{3,0,2,1:T(2,128)(2,1)} copy(bf16[2,1,29,128]{3,2,1,0:T(8,128)(2,1)S(1)} %shard_map.82) | data formatting | bytes 29696 | tf_op jit(solution)/shard_map/pallas_call | solution.py:287

commit v11 on v10

--- a/solution.py
+++ b/solution.py
@@ -55,6 +55,7 @@
     indices,
     spread,
     coeffs,
+    final_table,
     partial,
     outgoing,
     incoming,
@@ -118,9 +119,7 @@
     ]
     step_rows = ROWS_STEP * row_order
     stem_loads = [
-        pltpu.make_async_copy(
-            stem_hbm.at[half, 0], stem.at[half], stem_sem.at[half]
-        )
+        pltpu.make_async_copy(stem_hbm.at[half, 0], stem.at[half], stem_sem.at[half])
         for half in range(2)
     ]
     for load in small[:4] + stem_loads + small[4:]:
@@ -165,7 +164,9 @@
     for load in stem_loads + small[4:]:
         load.wait()
 
-    def mix(step):
+    steps = groups // ROWS_STEP
+
+    def mix_columns(step):
         rows = pl.ds(step * step_rows, step_rows)
         operand = jnp.concatenate([stem[0, rows, :], stem[1, rows, :]], 1)
         mixed = dot(operand, column_table).astype(BF16)
@@ -173,7 +174,10 @@
         for index in range(ROWS_STEP):
             piece = mixed[index * row_order : (index + 1) * row_order]
             pieces.append(jnp.concatenate([piece[:, :width], piece[:, width:]], 0))
-        result = dot(row_table, jnp.concatenate(pieces, 1))
+        return jnp.concatenate(pieces, 1)
+
+    def mix_rows(step, mixed):
+        result = dot(row_table, mixed)
         for index in range(ROWS_STEP):
             first = (step * ROWS_STEP + index) * heads
             spread[first : first + heads] = (
@@ -182,9 +186,14 @@
                 .astype(BF16)
             )
 
-    for step in range(groups // ROWS_STEP):
-        mix(step)
-
+    def mix(first, last, mixed):
+        for step in range(first, last):
+            later = mix_columns(step + 1) if step + 1 < steps else None
+            mix_rows(step, mixed)
+            mixed = later
+        return mixed
+
+    mixed = mix_columns(0)
     own = (iota((sub, order), 0) + me * sub == mode_labels[...]).astype(BF16)
     mode_real, mode_imag = dot(own, mode[0]), dot(own, mode[1])
     lane = iota((terms, span), 1)
@@ -192,20 +201,24 @@
         jnp.logical_or,
         [lane == iota((terms, span), 0) + place * terms for place in range(TILE)],
     ).astype(BF16)
+    mixed = mix(0, steps // 4, mixed)
+    halves = [
+        jnp.transpose(half).astype(BF16) for half in complex_rows(mode_real, mode_imag, 0)
+    ]
+    mixed = mix(steps // 4, steps // 2, mixed)
     blocks_of = jnp.concatenate(
-        [
-            dot(jnp.transpose(half).astype(BF16), repeat).reshape(row_blocks, fold, span)
-            for half in complex_rows(mode_real, mode_imag, 0)
-        ],
-        1,
-    )
+        [dot(half, repeat).reshape(row_blocks, fold, span) for half in halves], 1
+    )
+    mixed = mix(steps // 2, 3 * steps // 4, mixed)
     lane = iota(blocks_of.shape, 2)
     for place in range(TILE):
         inside = (lane >= place * terms) & (lane < (place + 1) * terms)
         coeffs[place] = jnp.where(inside, blocks_of, 0.0).astype(BF16)
-
-    final_real = jnp.concatenate([final[0], final[1]], 1)
-    final_imag = jnp.concatenate([-final[1], final[0]], 1)
+    final_table[0, :, :out_width] = final[0]
+    final_table[0, :, out_width:] = final[1]
+    final_table[1, :, :out_width] = -final[1]
+    final_table[1, :, out_width:] = final[0]
+    mix(3 * steps // 4, steps, mixed)
 
     for ask in asks:
         ask.wait_recv()
@@ -233,7 +246,7 @@
         ]
         real = jnp.concatenate(pieces[:fold], 1)
         imag = jnp.concatenate(pieces[fold:], 1)
-        return dot(real, final_real) + dot(imag, final_imag)
+        return dot(real, final_table[0]) + dot(imag, final_table[1])
 
     gives = [
         pltpu.make_async_remote_copy(
@@ -302,6 +315,7 @@
             pltpu.SMEM((2 * peers, width), jnp.int32),
             pltpu.VMEM((row_count // sub, terms, width), BF16),
             pltpu.VMEM((TILE, order // fold, 2 * fold, span), BF16),
+            pltpu.VMEM((2, fold * width, 2 * out_width), BF16),
             pltpu.VMEM((total * 2 * fold, width), F32),
             pltpu.VMEM((peers, padded, 2 * out_width), BF16),
             pltpu.VMEM((peers, padded, 2 * out_width), BF16),

time: 16.8 us -> 16.9 us (level)
  Pallas kernels: 16 us -> 16.2 us
    pallas_call x1, Pallas kernels: 16 us -> 16.2 us  [fused(): pl.pallas_call(functools.partial(fused_kernel, mode_size, group_size), ou...]
where the time goes in v11:
time: 16.9 us; the launch traced here: 16.8 us
  Pallas kernels  16.2 us (96%)
  local copies, waits for them, and re-layouts  0.61 us (4%)
    pallas_call x1, Pallas kernels, fused(): pl.pallas_call(functools.partial(fused_kernel, mode_size, group_size), ou...  16.2 us
    pallas_call x1, local copies, waits for them, and re-layouts, fused(): pl.pallas_call(functools.partial(fused_kernel, mode_size, group_size), ou...  0.61 us

profile of v11, /device:TPU:0, one launch (start us, length us, event | category | flops | bytes accessed | tf_op | source)
XLA Modules:
  0.0 16.8 jit_solution(5625256077772675914)
XLA Ops:
  0.0 16.2 %shard_map.82 = bf16[2,1,29,128]{3,2,1,0:T(8,128)(2,1)S(1)} custom-call(bf16[2,1,2048,128]{3,2,1,0:T(8,128)(2,1)} %stem_hbm.1, bf16[2,128,128]{2,1,0:T(8,128)(2,1)} %column_hbm.1, bf16[2,128,128]{2,1,0:T(8,128)(2,1)} %row_hbm.1, bf16[2,128,128]{2,1,0:T(8,128)(2,1)} %mode_hbm.1, bf16[2,1024,128]{2,1,0:T(8,128)(2,1)} %final_hbm.1, s32[1,128]{1,0:T(1,128)} %bitcast.2, ...), custom_call_target="tpu_custom_call" | custom-call | tf_op jit(solution)/shard_map/pallas_call | solution.py:300
  16.2 0.6 %copy.9 = bf16[2,1,29,128]{3,0,2,1:T(2,128)(2,1)} copy(bf16[2,1,29,128]{3,2,1,0:T(8,128)(2,1)S(1)} %shard_map.82) | data formatting | bytes 29696 | tf_op jit(solution)/shard_map/pallas_call | solution.py:300
